TPU v7x, 128 devices: a whole 4x4x4 slice. The times are simulated.
128 devices in a mesh: ctx: 4 (over z), ep: 32 (over y, x, core).
Axes of the slice: x: 4, y: 4, z: 4, core: 2. Of those that a mesh axis runs over, the one named last changes fastest.
Arguments:
- prefill_pages: bfloat16 [4, 32, 4, 20, 36864], P('ctx', 'ep'), may hold values from -4.5 to 4.5
- page_map: int32 [4, 32, 4, 20], P('ctx', 'ep'), may hold values from 0 to 79, as said below
- prompt_len: int32 [512], P(('ctx', 'ep')), may hold values from 1 to 1280, 393216 in all
- queries: bfloat16 [2, 512, 73728], P(None, ('ctx', 'ep')), may hold values from -24 to 24
- new_latent: bfloat16 [2, 512, 576], P(None, ('ctx', 'ep')), may hold values from -4 to 4
- resid: bfloat16 [2, 512, 7168], P(None, ('ctx', 'ep')), may hold values from -3 to 3
- w_uv: bfloat16 [128, 512, 128], P('ep'), may hold values from -1 to 1
- w_out: bfloat16 [16384, 7168], P('ep'), may hold values from -0.046875 to 0.046875
- norm_gain: bfloat16 [7168], replicated, may hold values from 0.099609375 to 1.8984375
- router_w: bfloat16 [7168, 32], replicated, may hold values from -0.0625 to 0.0625
- routes: int32 [2, 512, 8], P(None, ('ctx', 'ep')), may hold values from 0 to 31, all different within a row; in each aligned block of 4 rows (0 to 3, 4 to 7, ..., all dimensions but the last counted through in order) at most 2 rows name the same one
- w_gate: bfloat16 [32, 7168, 1024], P('ep', None, 'ctx'), may hold values from -0.0625 to 0.0625
- w_up: bfloat16 [32, 7168, 1024], P('ep', None, 'ctx'), may hold values from -0.0625 to 0.0625
- w_down: bfloat16 [32, 1024, 7168], P('ep', 'ctx'), may hold values from -0.1875 to 0.1875
Outputs:
- layer_out: bfloat16 [2, 512, 7168], P(None, ('ctx', 'ep'))
Inputs may be any that keep to these rules, and one draw needn't show every extreme that they name: For each owner ctx index c2 and column e, the values page_map[c2, e, c, s] over all c and s are the numbers 0 to 79, each once, and a value q * 20 + k at producer index c has k % 4 == c. `routes`: the 8 experts of a token differ. In each step the 4 tokens of one device name one expert at most 2 times.
All inputs are finite; a program needn't handle non-finite values. No bound on the sum of `prompt_len` on one device may be relied on, other than what follows from the above.
Results may differ from a plain program's by a relative error of at most 0.023.
Values may be sent and summed in bfloat16 or wider, within the bound.
A program may use at most 128 MiB of HBM per device.

v0:
```python
import jax
import jax.numpy as jnp
from jax import lax
from jax.sharding import PartitionSpec as P

LAT = 512
ROPE = 64
NOPE = 128
LATW = 576


norm_eps = 1e-06
route_scale = 2.5
masked_score = -1e30


def expert_ffn(rows, w_gate, w_up, w_down):
    row_shape = rows.shape
    flat_rows = rows.reshape(-1, row_shape[-1])
    gate_part = jnp.dot(flat_rows, w_gate[0], preferred_element_type=jnp.float32)
    up_part = jnp.dot(flat_rows, w_up[0], preferred_element_type=jnp.float32)
    hidden_units = (jax.nn.silu(gate_part) * up_part).astype(jnp.bfloat16)
    partial_out = jnp.dot(hidden_units, w_down[0], preferred_element_type=jnp.float32).astype(
        jnp.bfloat16
    )
    return partial_out.reshape(row_shape[:-1] + (w_down.shape[2],))


def per_device(
    prefill_pages,
    page_map,
    prompt_len,
    queries,
    new_latent,
    resid,
    w_uv,
    w_out,
    norm_gain,
    router_w,
    routes,
    w_gate,
    w_up,
    w_down,
):
    received = lax.all_to_all(prefill_pages, "ctx", split_axis=2, concat_axis=0, tiled=True)
    page_width = received.shape[-1]
    stacked = received.reshape(-1, page_width)
    targets = page_map.reshape(-1)
    requests = prompt_len.shape[0]
    placed = jnp.zeros_like(stacked).at[targets].set(stacked)
    page_cache = placed.reshape(requests, -1, LATW)
    key_count = page_cache.shape[1]
    steps_count = queries.shape[0]
    query_rows = queries.reshape(steps_count, requests, -1, LATW)
    score_scale = (NOPE + ROPE) ** (-0.5)
    old_scores = (
        jnp.einsum("sqhd,qld->qshl", query_rows, page_cache, preferred_element_type=jnp.float32)
        * score_scale
    )
    new_scores = (
        jnp.einsum("sqhd,jqd->qshj", query_rows, new_latent, preferred_element_type=jnp.float32)
        * score_scale
    )
    live_keys = jnp.arange(key_count)[None, :] < prompt_len[:, None]
    old_scores = jnp.where(live_keys[:, None, None, :], old_scores, masked_score)
    causal = jnp.arange(steps_count)[None, :] <= jnp.arange(steps_count)[:, None]
    new_scores = jnp.where(causal[None, :, None, :], new_scores, masked_score)
    row_max = jnp.maximum(old_scores.max(-1), new_scores.max(-1))[..., None]
    old_exp = jnp.exp(old_scores - row_max)
    new_exp = jnp.exp(new_scores - row_max)
    row_total = old_exp.sum(-1, keepdims=True) + new_exp.sum(-1, keepdims=True)
    old_weights = (old_exp / row_total).astype(jnp.bfloat16)
    new_weights = (new_exp / row_total).astype(jnp.bfloat16)
    mixed = jnp.einsum(
        "qshl,qlc->qshc", old_weights, page_cache[:, :, :LAT], preferred_element_type=jnp.float32
    )
    mixed = mixed + jnp.einsum(
        "qshj,jqc->qshc", new_weights, new_latent[:, :, :LAT], preferred_element_type=jnp.float32
    )
    attn_latent = mixed.astype(jnp.bfloat16)
    head_rows = lax.all_to_all(attn_latent, "ep", split_axis=2, concat_axis=0, tiled=True)
    head_out = jnp.einsum(
        "tshc,hcv->tshv", head_rows, w_uv, preferred_element_type=jnp.float32
    ).astype(jnp.bfloat16)
    flat_heads = head_out.reshape(head_out.shape[0] * steps_count, -1)
    attn_sum = lax.psum_scatter(
        jnp.dot(flat_heads, w_out, preferred_element_type=jnp.float32).astype(jnp.bfloat16),
        "ep",
        scatter_dimension=0,
        tiled=True,
    ).astype(jnp.float32)
    model_width = w_out.shape[1]
    hidden = jnp.swapaxes(resid, 0, 1).astype(jnp.float32) + attn_sum.reshape(
        requests, steps_count, model_width
    )
    mean_square = jnp.mean(hidden * hidden, axis=-1, keepdims=True)
    normed = (hidden * lax.rsqrt(mean_square + norm_eps) * norm_gain.astype(jnp.float32)).astype(
        jnp.bfloat16
    )
    expert_count = router_w.shape[1]
    affinity = jax.nn.sigmoid(
        jnp.einsum("qsd,de->qse", normed, router_w, preferred_element_type=jnp.float32)
    )
    route_rows = jnp.swapaxes(routes, 0, 1)
    top_count = route_rows.shape[2]
    picked = jnp.take_along_axis(affinity, route_rows, axis=2)
    gate_weights = route_scale * picked / jnp.sum(picked, axis=2, keepdims=True)
    one_hot = route_rows[..., None] == jnp.arange(expert_count)
    chosen = jnp.any(one_hot, axis=2)
    weight_table = jnp.sum(jnp.where(one_hot, gate_weights[..., None], 0.0), axis=2)
    chosen_count = chosen.astype(jnp.int32)
    rank = jnp.cumsum(chosen_count, axis=0) - chosen_count
    most_rows = max(2, (requests * top_count + expert_count - 1) // expert_count)
    capacity = steps_count * most_rows
    slot_index = jnp.arange(steps_count)[None, :, None] * most_rows + rank
    slot_hot = chosen[..., None] & (slot_index[..., None] == jnp.arange(capacity))
    send = jnp.einsum(
        "qsjm,qsd->jmd", slot_hot.astype(jnp.bfloat16), normed, preferred_element_type=jnp.float32
    ).astype(jnp.bfloat16)
    ctx_count = lax.axis_size("ctx")
    spread = jnp.broadcast_to(send[None], (ctx_count,) + send.shape).reshape(
        -1, capacity, model_width
    )
    partials = expert_ffn(
        lax.all_to_all(spread, ("ctx", "ep"), split_axis=0, concat_axis=0, tiled=True),
        w_gate,
        w_up,
        w_down,
    )
    returned = lax.all_to_all(partials, ("ctx", "ep"), split_axis=0, concat_axis=0, tiled=True)
    shard_terms = returned.reshape(ctx_count, expert_count, capacity, model_width).astype(
        jnp.float32
    )
    expert_out = jnp.sum(shard_terms, axis=0).astype(jnp.bfloat16)
    combine_table = slot_hot.astype(jnp.float32) * weight_table[..., None]
    routed = jnp.einsum(
        "qsjm,jmd->qsd",
        combine_table,
        expert_out.astype(jnp.float32),
        precision=lax.Precision.HIGHEST,
    )
    layer_out = (hidden + routed).astype(jnp.bfloat16)
    return jnp.swapaxes(layer_out, 0, 1)


def solution(mesh):
    placed = (
        P("ctx", "ep", None, None, None),
        P("ctx", "ep", None, None),
        P(("ctx", "ep")),
        P(None, ("ctx", "ep"), None),
        P(None, ("ctx", "ep"), None),
        P(None, ("ctx", "ep"), None),
        P("ep", None, None),
        P("ep", None),
        P(),
        P(),
        P(None, ("ctx", "ep"), None),
        P("ep", None, "ctx"),
        P("ep", None, "ctx"),
        P("ep", "ctx", None),
    )
    return jax.shard_map(
        per_device,
        mesh=mesh,
        in_specs=placed,
        out_specs=P(None, ("ctx", "ep"), None),
        check_vma=False,
    )
```

profile of v0, /device:TPU:1, one launch (start us, length us, event | category | flops | bytes accessed | tf_op | source)
XLA Modules:
  0.0 515.7 jit_solution(9314785790162808341)
XLA Ops:
  6.5 9.0 %copy.53 = bf16[1,1,4,20,36864]{4,3,1,0,2:T(8,128)(2,1)} copy(bf16[1,1,4,20,36864]{4,2,3,1,0:T(4,128)(2,1)} %param.14) | data formatting | bytes 11796480 | tf_op args[0]
  15.5 6.0 %all-to-all-start = ((bf16[1,1,4,20,36864]{4,3,1,0,2:T(8,128)(2,1)}), bf16[1,1,4,20,36864]{4,3,1,0,2:T(8,128)(2,1)}, u32[]{:S(2)}, u32[]{:S(2)}) async-start(bf16[1,1,4,20,36864]{4,3,1,0,2:T(8,128)(2,1)} %copy.53), calls=%async_computation | async-start | bytes 14155776 | tf_op jit(solution)/shard_map/all_to_all | solution.py:45
  21.5 0.5 reduce-scatter.2.cloned.1.call-start
  22.1 0.1 reshape.151
  22.1 1.3 reshape.154
  23.5 0.5 fusion.73
  24.0 0.1 iota_compare_fusion.1
  24.1 78.0 %all-to-all-done = bf16[1,1,4,20,36864]{4,3,1,0,2:T(8,128)(2,1)} async-done(((bf16[1,1,4,20,36864]{4,3,1,0,2:T(8,128)(2,1)}), bf16[1,1,4,20,36864]{4,3,1,0,2:T(8,128)(2,1)}, u32[]{:S(2)}, u32[]{:S(2)}) %all-to-all-start) | async-done | bytes 5898272 | tf_op jit(solution)/shard_map/all_to_all | solution.py:45
  102.1 5.4 %reshape.175 = bf16[80,36864]{1,0:T(8,128)(2,1)} reshape(bf16[1,1,4,20,36864]{4,3,1,0,2:T(8,128)(2,1)} %all-to-all-done) | data formatting | bytes 11796480 | tf_op jit(solution)/shard_map/reshape | solution.py:47
  107.5 13.5 %scatter_custom_fusion = bf16[80,36864]{1,0:T(8,128)(2,1)} fusion(s32[80]{0:T(128)S(1)} %fusion.67, bf16[80,36864]{1,0:T(8,128)(2,1)} %reshape.175, bf16[]{:T(256)} %constant.16.clone.1), kind=kCustom, calls=%fused_computation.25 | custom fusion | bytes 5898752 | tf_op jit(solution)/shard_map/scatter | solution.py:50
  121.0 12.0 %reshape.153 = bf16[4,1280,576]{2,1,0:T(8,128)(2,1)} reshape(bf16[80,36864]{1,0:T(8,128)(2,1)} %scatter_custom_fusion) | data formatting | bytes 11796480 | tf_op jit(solution)/shard_map/reshape | solution.py:51
  133.0 5.6 %bitcast_reduce_fusion = (f32[4,2,128]{2,1,0:T(2,128)S(1)}, f32[4,1280,2,128]{3,1,2,0:T(8,128)S(1)}) fusion(pred[4,1280]{1,0:T(4,128)(4,1)S(1)} %iota_compare_fusion.1, bf16[2,4,128,576]{3,2,1,0:T(8,128)(2,1)S(1)} %reshape.154, bf16[4,1280,576]{2,1,0:T(8,128)(2,1)} %reshape.153), kind=kOutput, calls=%fused_computation.15 | convolution fusion | flops 1513880576 | bytes 12329984 | tf_op jit(solution)/shard_map/sqhd,qld->qshl/dot_general | solution.py:57
  138.7 1.5 fusion.8
  140.2 3.8 fusion.6
  144.0 0.5 add_convert_fusion
  144.5 1.1 copy.60
  145.6 25.4 %all_to_all.37 = bf16[4,2,128,512]{3,1,0,2:T(2,128)(2,1)S(1)} all-to-all(bf16[4,2,128,512]{3,1,0,2:T(2,128)(2,1)S(1)} %copy.60), channel_id=1, replica_groups=mesh['ctx'=4,'ep'=32] {'ep'}, dimensions={2} | all-to-all | bytes 2097152 | tf_op jit(solution)/shard_map/all_to_all | solution.py:81
  171.0 0.4 copy.128
  171.4 0.3 all_to_all.30
  171.7 0.4 fusion.29
  172.1 0.2 copy.62
  172.4 7.0 %convolution_convert_fusion.1 = bf16[256,7168]{1,0:T(8,128)(2,1)} fusion(bf16[512,7168]{1,0:T(8,128)(2,1)} %param.21, bf16[32,8,4,128]{3,2,1,0:T(4,128)(2,1)S(1)} %bitcast.121), kind=kOutput, calls=%fused_computation.3 | convolution fusion | flops 1880883200 | bytes 11272192 | tf_op jit(solution)/shard_map/dot_general | solution.py:87
  179.4 0.0 reduce-scatter.2.cloned.1.call-update
  179.4 0.1 fusion.51
  179.5 0.1 fusion.39
  179.6 74.6 %reduce-scatter.2.cloned.1.call-done = bf16[8,7168]{1,0:T(8,128)(2,1)} async-done(((bf16[256,7168]{1,0:T(8,128)(2,1)}), bf16[8,7168]{1,0:T(8,128)(2,1)}) %reduce-scatter.2.cloned.1.call-update) | async-done | bytes 114704 | tf_op jit(solution)/shard_map/reduce_scatter | solution.py:86
  254.2 1.1 reshape.164
  255.3 0.2 multiply_reduce_fusion
  255.5 0.1 multiply_convert_fusion
  255.6 0.7 fusion
  256.3 1.4 copy.68
  257.8 5.3 %broadcast_in_dim.78 = bf16[4,32,4,7168]{3,2,1,0:T(4,128)(2,1)} broadcast(bf16[32,4,7168]{2,1,0:T(4,128)(2,1)S(1)} %copy.68), dimensions={1,2,3} | broadcast | bytes 9175040 | tf_op jit(solution)/shard_map/broadcast_in_dim | solution.py:121
  263.0 96.1 %all_to_all.38 = bf16[128,4,7168]{2,1,0:T(4,128)(2,1)} all-to-all(bf16[128,4,7168]{2,1,0:T(4,128)(2,1)} %bitcast.118), channel_id=1, replica_groups=mesh['ctx'=4,'ep'=32] {'ctx','ep'}, dimensions={0} | all-to-all | bytes 14680064 | tf_op jit(solution)/shard_map/all_to_all | solution.py:125
  359.2 12.1 %reshape.160 = bf16[512,7168]{1,0:T(8,128)(2,1)} reshape(bf16[128,4,7168]{2,1,0:T(4,128)(2,1)} %all_to_all.38) | data formatting | bytes 14680064 | tf_op jit(solution)/shard_map/reshape | solution.py:19
  371.3 6.2 %fusion.12 = f32[512,256]{1,0:T(8,128)S(1)} fusion(bf16[512,7168]{1,0:T(8,128)(2,1)} %reshape.160, bf16[1,7168,256]{2,1,0:T(8,128)(2,1)} %param.25), kind=kOutput, calls=%fused_computation.23 | convolution fusion | flops 1879048192 | bytes 11534336 | tf_op jit(solution)/shard_map/dot_general | solution.py:20
  377.5 16.0 %convolution_convert_fusion = bf16[512,7168]{1,0:T(8,128)(2,1)} fusion(bf16[1,256,7168]{2,1,0:T(8,128)(2,1)} %param.27, bf16[512,7168]{1,0:T(8,128)(2,1)} %reshape.160, bf16[1,7168,256]{2,1,0:T(8,128)(2,1)} %param.26, f32[512,256]{1,0:T(8,128)S(1)} %fusion.12), kind=kOutput, calls=%fused_computation.2 | convolution fusion | flops 3762552832 | bytes 22544384 | tf_op jit(solution)/shard_map/dot_general | solution.py:23
  393.4 12.6 %reshape.161 = bf16[128,4,7168]{2,1,0:T(4,128)(2,1)} reshape(bf16[512,7168]{1,0:T(8,128)(2,1)} %convolution_convert_fusion) | data formatting | bytes 14680064 | tf_op jit(solution)/shard_map/reshape | solution.py:26
  406.0 6.3 %all-to-all-start.3 = ((bf16[128,4,7168]{2,1,0:T(4,128)(2,1)}), bf16[128,4,7168]{2,1,0:T(4,128)(2,1)}, u32[]{:S(2)}, u32[]{:S(2)}) async-start(bf16[128,4,7168]{2,1,0:T(4,128)(2,1)} %reshape.161), calls=%async_computation.4 | async-start | bytes 14680064 | tf_op jit(solution)/shard_map/all_to_all | solution.py:130
  412.3 0.1 reshape.165
  412.4 0.3 fusion.42
  412.7 1.0 gather_fusion
  413.7 0.1 reshape.168
  413.8 0.1 fusion.72
  413.9 0.1 multiply_divide_fusion
  414.0 0.1 select_reduce_fusion
  414.1 85.1 %all-to-all-done.3 = bf16[128,4,7168]{2,1,0:T(4,128)(2,1)} async-done(((bf16[128,4,7168]{2,1,0:T(4,128)(2,1)}), bf16[128,4,7168]{2,1,0:T(4,128)(2,1)}, u32[]{:S(2)}, u32[]{:S(2)}) %all-to-all-start.3) | async-done | bytes 7340064 | tf_op jit(solution)/shard_map/all_to_all | solution.py:130
  499.2 7.5 %reduce_sum.62 = bf16[32,4,7168]{2,1,0:T(4,128)(2,1)S(1)} reduce(bf16[4,32,4,7168]{3,2,1,0:T(4,128)(2,1)} %bitcast.24, bf16[]{:T(256)} %constant.16.clone.1), dimensions={0}, to_apply=%region_11.12 | reduce | flops 2752512 | bytes 9175042 | tf_op jit(solution)/shard_map/reduce_sum | solution.py:134
  506.7 1.9 fusion.3
  (36 shorter events, 0.2 us)
Async XLA Ops:
  6.5 165.1 %copy-start = (bf16[4,512,128]{2,1,0:T(8,128)(2,1)S(1)}, bf16[4,512,128]{2,1,0:T(8,128)(2,1)}, u32[]{:S(2)}) copy-start(bf16[4,512,128]{2,1,0:T(8,128)(2,1)} %param.20) | copy-start | bytes 1572868
  15.5 6.5 %copy-start.8 = (s32[1,1,4,20]{3,2,1,0:T(4,128)S(1)}, s32[1,1,4,20]{3,2,1,0:T(4,128)}, u32[]{:S(2)}) copy-start(s32[1,1,4,20]{3,2,1,0:T(4,128)} %param.15) | copy-start | bytes 964
  15.5 6.6 %copy-start.3 = (bf16[2,4,73728]{2,1,0:T(4,128)(2,1)S(1)}, bf16[2,4,73728]{2,1,0:T(4,128)(2,1)}, u32[]{:S(2)}) copy-start(bf16[2,4,73728]{2,1,0:T(4,128)(2,1)} %param.17) | copy-start | bytes 3538948
  15.5 8.0 %copy-start.7 = (bf16[2,4,576]{2,1,0:T(4,128)(2,1)S(1)}, bf16[2,4,576]{2,1,0:T(4,128)(2,1)}, u32[]{:S(2)}) copy-start(bf16[2,4,576]{2,1,0:T(4,128)(2,1)} %param.18) | copy-start | bytes 27652
  15.5 8.5 %copy-start.9 = (s32[4]{0:T(128)S(1)}, s32[4]{0:T(128)}, u32[]{:S(2)}) copy-start(s32[4]{0:T(128)} %param.16) | copy-start | bytes 52
  15.5 86.5 %all-to-all-start = ((bf16[1,1,4,20,36864]{4,3,1,0,2:T(8,128)(2,1)}), bf16[1,1,4,20,36864]{4,3,1,0,2:T(8,128)(2,1)}, u32[]{:S(2)}, u32[]{:S(2)}) async-start(bf16[1,1,4,20,36864]{4,3,1,0,2:T(8,128)(2,1)} %copy.53), calls=%async_computation | async-start | bytes 14155776 | tf_op jit(solution)/shard_map/all_to_all | solution.py:45
  21.5 232.7 %reduce-scatter.2.cloned.1.call-start = ((), (), s32[]{:S(2)}) async-start(), calls=%async_computation.5 | async-start | bytes 3784704 | tf_op jit(solution)/shard_map/reduce_scatter | solution.py:86
  133.0 7.2 %copy-start.2 = (bf16[4,1280,576]{2,1,0:T(8,128)(2,1)S(1)}, bf16[4,1280,576]{2,1,0:T(8,128)(2,1)}, u32[]{:S(2)}) copy-start(bf16[4,1280,576]{2,1,0:T(8,128)(2,1)} %reshape.153) | copy-start | bytes 17694724
  172.3 7.1 %copy-start.6 = (bf16[7168]{0:T(1024)(128)(2,1)S(1)}, bf16[7168]{0:T(1024)(128)(2,1)}, u32[]{:S(2)}) copy-start(bf16[7168]{0:T(1024)(128)(2,1)} %param.22) | copy-start | bytes 43012
  172.3 7.1 %copy-start.5 = (s32[2,4,8]{2,1,0:T(4,128)S(1)}, s32[2,4,8]{2,1,0:T(4,128)}, u32[]{:S(2)}) copy-start(s32[2,4,8]{2,1,0:T(4,128)} %param.24) | copy-start | bytes 772
  172.4 82.9 %copy-start.4 = (bf16[2,4,7168]{2,1,0:T(4,128)(2,1)S(1)}, bf16[2,4,7168]{2,1,0:T(4,128)(2,1)}, u32[]{:S(2)}) copy-start(bf16[2,4,7168]{2,1,0:T(4,128)(2,1)} %param.19) | copy-start | bytes 344068
  406.0 6.4 %copy-start.10 = (bf16[7168,32]{0,1:T(8,128)(2,1)S(1)}, bf16[7168,32]{0,1:T(8,128)(2,1)}, u32[]{:S(2)}) copy-start(bf16[7168,32]{0,1:T(8,128)(2,1)} %param.23) | copy-start | bytes 1376260
  406.0 93.1 %all-to-all-start.3 = ((bf16[128,4,7168]{2,1,0:T(4,128)(2,1)}), bf16[128,4,7168]{2,1,0:T(4,128)(2,1)}, u32[]{:S(2)}, u32[]{:S(2)}) async-start(bf16[128,4,7168]{2,1,0:T(4,128)(2,1)} %reshape.161), calls=%async_computation.4 | async-start | bytes 14680064 | tf_op jit(solution)/shard_map/all_to_all | solution.py:130
  499.2 9.4 %copy-start.1 = (bf16[4,512,128]{2,1,0:T(8,128)(2,1)S(1)}, bf16[4,512,128]{2,1,0:T(8,128)(2,1)}, u32[]{:S(2)}) copy-start(bf16[4,512,128]{2,1,0:T(8,128)(2,1)} %param.20) | copy-start | bytes 1572868
Sparse Core Ops, SparseCore 0:
  179.5 74.6 reduce-scatter.1
where the time goes:
time: 520 us; the launch traced here: 516 us
  waiting for transfers between devices  238 us (46%)
  blocking collectives  122 us (23%)
  local copies, waits for them, and re-layouts  77 us (15%)
  matrix products  42.8 us (8%)
  between operations  14 us (3%)
  starting transfers between devices  12.8 us (2%)
  other arithmetic  9.92 us (2%)
    all_to_all x1, blocking collectives, per_device(): lax.all_to_all(spread, ('ctx', 'ep'), split_axis=0, concat_axis=0, tiled=...  96.1 us
    all_to_all x1, waiting for transfers between devices, per_device(): lax.all_to_all(partials, ('ctx', 'ep'), split_axis=0, concat_axis=0, tile...  85.1 us
    all_to_all x1, waiting for transfers between devices, per_device(): lax.all_to_all(prefill_pages, 'ctx', split_axis=2, concat_axis=0, tiled=T...  78 us
    reduce_scatter x1, waiting for transfers between devices, per_device(): lax.psum_scatter(jnp.dot(flat_heads, w_out, preferred_element_type=jnp.fl...  74.6 us
    all_to_all x1, blocking collectives, per_device(): lax.all_to_all(attn_latent, 'ep', split_axis=2, concat_axis=0, tiled=True)  25.4 us
    dot_general x1, matrix products, expert_ffn(): jnp.dot(hidden_units, w_down[0], preferred_element_type=jnp.float32)  16 us
    scatter x1, local copies, waits for them, and re-layouts, per_device(): placed = jnp.zeros_like(stacked).at[targets].set(stacked)  13.5 us
    reshape x1, local copies, waits for them, and re-layouts, expert_ffn(): return partial_out.reshape(row_shape[:-1] + (w_down.shape[2],))  12.6 us
  transfers between devices with their start and end apart: 3, of which 3 were waited for; matrix products, arithmetic and copies ran while one was open for 1% of the time, Pallas kernels for 0%

commit v1 on v0

v1 whole, which is shorter than its diff:
```python
import jax
import jax.numpy as jnp
from jax import lax
from jax.experimental import pallas as pl
from jax.experimental.pallas import tpu as pltpu
from jax.sharding import PartitionSpec as P

LAT = 512
ROPE = 64
NOPE = 128
LATW = 576


norm_eps = 1e-06
route_scale = 2.5
masked_score = -1e30

HALF = 3584
GW = HALF + 128
MESH_IDS = pl.DeviceIdType.MESH
AG_PARTS = ((0, 640, 640), (1280, 640, 640), (2560, 640, 512))
RS_PARTS = ((0, 640, 512), (1152, 640, 512), (2304, 640, 640))
PLANE_PARTS = ((0, 896, 896), (1792, 896, 896))
COPIES = 160


class Links:
    def __init__(self, send_sem, recv_sem):
        self.send_sem, self.recv_sem, self.used = send_sem, recv_sem, 0
        self.z, ep = lax.axis_index("ctx"), lax.axis_index("ep")
        self.core = lax.rem(ep, 2)
        self.y, self.x = ep // 8, lax.rem(ep // 2, 4)
        self.ep = ep
        self.coords = (self.z, self.y, self.x)

    def shifted(self, axis, step):
        return lax.rem(self.coords[axis] + (step % 4), 4)

    def neighbour(self, axis, step):
        c = list(self.coords)
        c[axis] = self.shifted(axis, step)
        return (c[0], (c[1] * 4 + c[2]) * 2 + self.core)

    def partner(self):
        return (self.z, self.ep + 1 - 2 * self.core)

    def send(self, src, dst, device, landing):
        k = self.used
        self.used += 1
        make = lambda s, d: pltpu.make_async_remote_copy(
            src_ref=s,
            dst_ref=d,
            send_sem=self.send_sem.at[k],
            recv_sem=self.recv_sem.at[k],
            device_id=device,
            device_id_type=MESH_IDS,
        )
        out = make(src, dst)
        out.start()
        return out, make(landing, landing)


def wait_in(copies):
    for _, incoming in copies:
        incoming.wait_recv()


def wait_out(copies):
    for outgoing, _ in copies:
        outgoing.wait_send()


def pick(ref, chosen, start, width):
    index = tuple(chosen.get(a, slice(None)) for a in range(len(ref.shape) - 2))
    return ref.at[index + (slice(None), pl.ds(start, width))]


def gather_blocks(link, held, pushed):
    sent, pushes = [], []

    def push(part, axis, coord):
        start, wa, wb = AG_PARTS[part]
        src = pick(held, {axis: coord}, start, wa + wb)
        dst = pick(pushed, {axis: coord}, start, wa + wb)
        pushes.append(link.send(src, dst, link.partner(), dst))

    for stage in range(3):
        first = []
        for p, (start, wa, wb) in enumerate(AG_PARTS):
            order = [(p + j) % 3 for j in range(3)]
            axis = order[stage]
            rest = {a: link.coords[a] for a in order[stage + 1 :]}
            mine = pick(held, {**rest, axis: link.coords[axis]}, start, wa + wb)
            below = pick(held, {**rest, axis: link.shifted(axis, -1)}, start, wa + wb)
            above = pick(held, {**rest, axis: link.shifted(axis, 1)}, start, wa + wb)
            first.append(
                (
                    link.send(mine, mine, link.neighbour(axis, 1), below),
                    link.send(mine, mine, link.neighbour(axis, -1), above),
                )
            )
            if stage == 2:
                push(p, axis, link.coords[axis])
        second = []
        for p, (start, wa, wb) in enumerate(AG_PARTS):
            order = [(p + j) % 3 for j in range(3)]
            axis = order[stage]
            rest = {a: link.coords[a] for a in order[stage + 1 :]}
            wait_in(first[p])
            up = pick(held, {**rest, axis: link.shifted(axis, -1)}, start, wa)
            down = pick(held, {**rest, axis: link.shifted(axis, 1)}, start + wa, wb)
            far_a = pick(held, {**rest, axis: link.shifted(axis, 2)}, start, wa)
            far_b = pick(held, {**rest, axis: link.shifted(axis, 2)}, start + wa, wb)
            second.append(
                (
                    link.send(up, up, link.neighbour(axis, 1), far_a),
                    link.send(down, down, link.neighbour(axis, -1), far_b),
                )
            )
            if stage == 2:
                push(p, axis, link.shifted(axis, -1))
                push(p, axis, link.shifted(axis, 1))
        for p in range(3):
            wait_in(second[p])
            if stage == 2:
                push(p, (p + 2) % 3, link.shifted((p + 2) % 3, 2))
            sent += list(first[p]) + list(second[p])
    return sent, pushes


def scatter_sums(link, parts, axes, sums, landings, last):
    sent = []
    count = len(axes)
    for stage in range(count):
        far_in, low_in, high_in = landings[stage]
        steps = []
        for p, (start, wa, wb) in enumerate(parts):
            order = [axes[(p + j) % count] for j in range(count)]
            axis = order[stage]
            done = {a: link.coords[a] for a in order[:stage]}
            at = lambda coord, lo, w, done=done, axis=axis: pick(
                sums, {k - axes[0]: v for k, v in {**done, axis: coord}.items()}, lo, w
            )
            land = lambda ref, lo, w: ref.at[(slice(None),) * (count - stage) + (pl.ds(lo, w),)]
            far = link.shifted(axis, 2)
            la, lb = land(far_in, start, wa), land(far_in, start + wa, wb)
            steps.append(
                (
                    at,
                    land,
                    axis,
                    (
                        link.send(at(far, start, wa), la, link.neighbour(axis, 1), la),
                        link.send(at(far, start + wa, wb), lb, link.neighbour(axis, -1), lb),
                    ),
                )
            )
        final = []
        for p, (start, wa, wb) in enumerate(parts):
            at, land, axis, first = steps[p]
            wait_in(first)
            up, down = link.shifted(axis, 1), link.shifted(axis, -1)
            for coord, lo, w in ((up, start, wa), (down, start + wa, wb)):
                view, got = at(coord, lo, w), land(far_in, lo, w)
                view[...] = (
                    view[...].astype(jnp.float32) + got[...].astype(jnp.float32)
                ).astype(jnp.bfloat16)
            low, high = land(low_in, start, wa + wb), land(high_in, start, wa + wb)
            second = (
                link.send(at(up, start, wa + wb), low, link.neighbour(axis, 1), low),
                link.send(at(down, start, wa + wb), high, link.neighbour(axis, -1), high),
            )
            final.append((at(link.coords[axis], start, wa + wb), low, high, second))
            sent += list(first) + list(second)
        for p, (start, wa, wb) in enumerate(parts):
            view, low, high, second = final[p]
            wait_in(second)
            total = (
                view[...].astype(jnp.float32)
                + low[...].astype(jnp.float32)
                + high[...].astype(jnp.float32)
            )
            if stage == count - 1:
                last(start, wa + wb, total)
            else:
                view[...] = total.astype(jnp.bfloat16)
    return sent


def layer_kernel(
    heads_ref,
    w_uv_ref,
    resid_ref,
    chosen_ref,
    gain_ref,
    router_ref,
    w_out_hbm,
    w_gate_hbm,
    w_up_hbm,
    w_down_hbm,
    out_ref,
    big,
    wg,
    wu,
    wd,
    flat,
    part_send,
    part_land,
    part_sum,
    plane_a0,
    plane_a1,
    plane_b0,
    plane_b1,
    plane_c0,
    plane_c1,
    hid,
    picked,
    stat_out,
    stat_in,
    held,
    pushed,
    gate_acc,
    up_acc,
    units,
    far0,
    low0,
    high0,
    far1,
    low1,
    high1,
    far2,
    low2,
    high2,
    fin,
    fin_in,
    send_sem,
    recv_sem,
    load_sem,
):
    link = Links(send_sem, recv_sem)
    core = link.core
    other = 1 - core
    partner = link.partner()
    f32, bf16 = jnp.float32, jnp.bfloat16

    own_cols = pl.ds(pl.multiple_of(core * HALF, 128), HALF)
    other_cols = pl.ds(pl.multiple_of(other * HALF, 128), HALF)
    loads = []

    def load(src, dst):
        copy = pltpu.make_async_copy(src, dst, load_sem.at[len(loads)])
        copy.start()
        loads.append(copy)

    load(w_out_hbm.at[:, :, :, :, other_cols], big.at[pl.ds(2, 2)])
    load(w_out_hbm.at[:, :, :, :, own_cols], big.at[pl.ds(0, 2)])
    for slot, cols in ((0, own_cols), (1, other_cols)):
        load(w_gate_hbm.at[cols], wg.at[slot])
        load(w_up_hbm.at[cols], wu.at[slot])
        load(w_down_hbm.at[:, cols], wd.at[slot])

    barrier = pltpu.get_barrier_semaphore()
    for axis in range(3):
        for step in (1, -1):
            pl.semaphore_signal(
                barrier, inc=1, device_id=link.neighbour(axis, step), device_id_type=MESH_IDS
            )
    pl.semaphore_signal(barrier, inc=1, device_id=partner, device_id_type=MESH_IDS)
    pl.semaphore_wait(barrier, 7)

    sent = []
    swaps = [
        link.send(resid_ref.at[other], hid.at[core], partner, hid.at[other]),
        link.send(chosen_ref, picked.at[core], partner, picked.at[other]),
    ]
    sent += swaps

    for pair in range(2):
        rows = heads_ref[:, pl.ds(pair * 16, 16), :].reshape(512, LAT)
        for one in range(2):
            head = 2 * pair + one
            value = jnp.dot(rows, w_uv_ref[head], preferred_element_type=f32)
            value = value.reshape(32, 2, 8, 128)[:, one].reshape(256, 128)
            flat[:, pl.ds(head * 128, 128)] = value.astype(bf16)

    def project(slot, start):
        lanes = pl.ds(start, 256)
        weight = big[pl.ds(2 * slot, 2), :, :, :, lanes].reshape(512, 256)
        value = jnp.dot(flat[...], weight, preferred_element_type=f32)
        return value.reshape(4, 4, 16, 256)

    loads[0].wait()
    core_swap = []
    for start in (0, 1792):

        @pl.loop(0, 7)
        def _(j, start=start):
            at = pl.multiple_of(start + j * 256, 256)
            part_send[:, :, :, pl.ds(at, 256)] = project(1, at).astype(bf16)

        lanes = pl.ds(start, 1792)
        dst = part_land.at[:, :, :, lanes]
        core_swap.append(link.send(part_send.at[:, :, :, lanes], dst, partner, dst))
    sent += core_swap
    loads[1].wait()
    for turn, start in enumerate((0, 1792)):
        wait_in(core_swap[turn : turn + 1])

        @pl.loop(0, 7)
        def _(j, start=start):
            at = pl.multiple_of(start + j * 256, 256)
            value = project(0, at) + part_land[:, :, :, pl.ds(at, 256)].astype(f32)
            part_sum[:, :, :, pl.ds(at, 256)] = value.astype(bf16)

    hid[core] = resid_ref[core]
    picked[core] = chosen_ref[...]
    wait_in(swaps)

    def add_hidden(start, width, total):
        lanes = pl.ds(start, width)
        hid[:, :, lanes] = hid[:, :, lanes] + total.reshape(2, 8, width)

    sent += scatter_sums(
        link,
        PLANE_PARTS,
        (1, 2),
        part_sum,
        ((plane_a0, plane_b0, plane_c0), (plane_a1, plane_b1, plane_c1)),
        add_hidden,
    )

    hidden = hid[...].reshape(16, HALF)
    gain = gain_ref[core]
    logits = jnp.dot(
        (hidden * gain).astype(bf16), router_ref[core], preferred_element_type=f32
    )
    squares = jnp.sum(hidden * hidden, axis=1, keepdims=True)
    lane = lax.broadcasted_iota(jnp.int32, (16, 128), 1)
    mine = jnp.where(lane < 64, logits, jnp.broadcast_to(squares, (16, 128)))
    stat_out[...] = mine
    stat = link.send(stat_out, stat_in, partner, stat_in)
    sent.append(stat)
    wait_in([stat])
    both = mine + stat_in[...]
    scale = lax.rsqrt(both[:, 64:65] / (2 * HALF) + norm_eps)
    affinity = jax.nn.sigmoid(both * scale) * picked[...].reshape(16, 128)
    weights = route_scale * affinity / jnp.sum(affinity, axis=1, keepdims=True)
    high = weights.astype(bf16)
    low = (weights - high.astype(f32)).astype(bf16).astype(f32)
    table = high.astype(f32) + pltpu.roll(low, 32, axis=1)
    normed = (hid[...].reshape(16, HALF) * scale * gain).astype(bf16)
    held[link.z, link.y, link.x, :, pl.ds(0, HALF)] = normed
    held[link.z, link.y, link.x, :, pl.ds(HALF, 128)] = table.astype(bf16)

    gathers, pushes = gather_blocks(link, held, pushed)

    for copy in loads[2:]:
        copy.wait()

    def own_half(i, carry):
        rows = held[i, :, :, :, pl.ds(0, HALF)].reshape(256, HALF)
        gate_acc[i] = jnp.dot(rows, wg[0], preferred_element_type=f32)
        up_acc[i] = jnp.dot(rows, wu[0], preferred_element_type=f32)
        return carry

    lax.fori_loop(0, 4, own_half, 0)
    wait_in(pushes)

    def other_half(i, carry):
        rows = pushed[i, :, :, :, pl.ds(0, HALF)].reshape(256, HALF)
        gate_part = gate_acc[i] + jnp.dot(rows, wg[1], preferred_element_type=f32)
        up_part = up_acc[i] + jnp.dot(rows, wu[1], preferred_element_type=f32)
        table = held[i, :, :, :, pl.ds(HALF, 128)].reshape(256, 128).astype(f32)
        lane = lax.broadcasted_iota(jnp.int32, (256, 128), 1)
        here = (lane == link.ep) | (lane == link.ep + 32)
        factor = jnp.sum(jnp.where(here, table, 0.0), axis=1, keepdims=True)
        units[i] = (jax.nn.silu(gate_part) * up_part * factor).astype(bf16)
        return carry

    lax.fori_loop(0, 4, other_half, 0)
    wait_out(gathers + pushes)

    back = []
    for i in range(4):

        @pl.loop(0, 7)
        def _(j, i=i):
            lanes = pl.ds(pl.multiple_of(j * 512, 512), 512)
            value = jnp.dot(units[i], wd[1, :, lanes], preferred_element_type=f32)
            pushed[i, :, :, :, lanes] = value.astype(bf16).reshape(4, 4, 16, 512)

        dst = big.at[i]
        back.append(link.send(pushed.at[i, :, :, :, pl.ds(0, HALF)], dst, partner, dst))
    for i in range(4):
        wait_in(back[i : i + 1])

        @pl.loop(0, 7)
        def _(j, i=i):
            lanes = pl.ds(pl.multiple_of(j * 512, 512), 512)
            value = jnp.dot(units[i], wd[0, :, lanes], preferred_element_type=f32)
            value = value.reshape(4, 4, 16, 512) + big[i, :, :, :, lanes].astype(f32)
            held[i, :, :, :, lanes] = value.astype(bf16)

    sent += back

    def add_routed(start, width, total):
        lanes = pl.ds(start, width)
        fin[:, :, lanes] = hid[:, :, lanes] + total.reshape(2, 8, width)

    sent += scatter_sums(
        link,
        RS_PARTS,
        (0, 1, 2),
        held,
        ((far0, low0, high0), (far1, low1, high1), (far2, low2, high2)),
        add_routed,
    )
    swap = link.send(fin.at[other], fin_in, partner, fin_in)
    sent.append(swap)
    out_ref[core] = fin[core]
    wait_in([swap])
    out_ref[other] = fin_in[...]
    wait_out(sent)


def layer_call(head_rows, w_uv, resid_halves, chosen, gain, router, w_out, w_gate, w_up, w_down):
    vmem, hbm = pl.BlockSpec(memory_space=pltpu.VMEM), pl.BlockSpec(memory_space=pl.ANY)
    bf16, f32 = jnp.bfloat16, jnp.float32

    def block(*lead, lanes=HALF, kind=bf16):
        return pltpu.VMEM(lead + (lanes,), kind)

    plane = [block(4, 16), block(16)] * 3
    torus = [block(4, 4, 16)] * 3 + [block(4, 16)] * 3 + [block(16)] * 3
    scratch = (
        [block(4, 4, 4, 16)]
        + [pltpu.VMEM((2, HALF, 256), bf16)] * 2
        + [pltpu.VMEM((2, 256, HALF), bf16), pltpu.VMEM((256, 512), bf16)]
        + [block(4, 4, 16)] * 3
        + plane
        + [block(2, 8, kind=f32), pltpu.VMEM((2, 8, 128), f32)]
        + [pltpu.VMEM((16, 128), f32)] * 2
        + [block(4, 4, 4, 16, lanes=GW)] * 2
        + [pltpu.VMEM((4, 256, 256), f32)] * 2
        + [pltpu.VMEM((4, 256, 256), bf16)]
        + torus
        + [block(2, 8, kind=f32), block(8, kind=f32)]
        + [pltpu.SemaphoreType.DMA((COPIES,))] * 2
        + [pltpu.SemaphoreType.DMA((8,))]
    )
    return pl.pallas_call(
        layer_kernel,
        out_shape=jax.ShapeDtypeStruct((2, 8, HALF), f32),
        in_specs=[vmem] * 6 + [hbm] * 4,
        out_specs=vmem,
        scratch_shapes=scratch,
        compiler_params=pltpu.CompilerParams(
            collective_id=1, has_side_effects=True, vmem_limit_bytes=62 * 1024 * 1024
        ),
        cost_estimate=pl.CostEstimate(
            flops=20_000_000_000, bytes_accessed=22_000_000, transcendentals=300_000
        ),
        name="layer",
    )(head_rows, w_uv, resid_halves, chosen, gain, router, w_out, w_gate, w_up, w_down)


def layer_operands(resid, routes, w_out, norm_gain, router_w, w_gate, w_up, w_down):
    resid_halves = jnp.swapaxes(resid.reshape(8, 2, HALF), 0, 1).astype(jnp.float32)
    route_rows = routes.reshape(8, -1)
    chosen = jnp.any(route_rows[..., None] == jnp.arange(128), axis=1).astype(jnp.float32)
    gain = norm_gain.astype(jnp.float32).reshape(2, 1, HALF)
    router = jnp.pad(router_w, ((0, 0), (0, 128 - router_w.shape[1]))).reshape(2, HALF, 128)
    return (
        resid_halves,
        chosen,
        gain,
        router,
        w_out.reshape(2, 4, 4, 16, 2 * HALF),
        w_gate[0],
        w_up[0],
        w_down[0],
    )


def per_device(
    prefill_pages,
    page_map,
    prompt_len,
    queries,
    new_latent,
    resid,
    w_uv,
    w_out,
    norm_gain,
    router_w,
    routes,
    w_gate,
    w_up,
    w_down,
):
    received = lax.all_to_all(prefill_pages, "ctx", split_axis=2, concat_axis=0, tiled=True)
    page_width = received.shape[-1]
    stacked = received.reshape(-1, page_width)
    targets = page_map.reshape(-1)
    requests = prompt_len.shape[0]
    placed = jnp.zeros_like(stacked).at[targets].set(stacked)
    page_cache = placed.reshape(requests, -1, LATW)
    key_count = page_cache.shape[1]
    steps_count = queries.shape[0]
    query_rows = queries.reshape(steps_count, requests, -1, LATW)
    score_scale = (NOPE + ROPE) ** (-0.5)
    old_scores = (
        jnp.einsum("sqhd,qld->qshl", query_rows, page_cache, preferred_element_type=jnp.float32)
        * score_scale
    )
    new_scores = (
        jnp.einsum("sqhd,jqd->qshj", query_rows, new_latent, preferred_element_type=jnp.float32)
        * score_scale
    )
    live_keys = jnp.arange(key_count)[None, :] < prompt_len[:, None]
    old_scores = jnp.where(live_keys[:, None, None, :], old_scores, masked_score)
    causal = jnp.arange(steps_count)[None, :] <= jnp.arange(steps_count)[:, None]
    new_scores = jnp.where(causal[None, :, None, :], new_scores, masked_score)
    row_max = jnp.maximum(old_scores.max(-1), new_scores.max(-1))[..., None]
    old_exp = jnp.exp(old_scores - row_max)
    new_exp = jnp.exp(new_scores - row_max)
    row_total = old_exp.sum(-1, keepdims=True) + new_exp.sum(-1, keepdims=True)
    old_weights = (old_exp / row_total).astype(jnp.bfloat16)
    new_weights = (new_exp / row_total).astype(jnp.bfloat16)
    mixed = jnp.einsum(
        "qshl,qlc->qshc", old_weights, page_cache[:, :, :LAT], preferred_element_type=jnp.float32
    )
    mixed = mixed + jnp.einsum(
        "qshj,jqc->qshc", new_weights, new_latent[:, :, :LAT], preferred_element_type=jnp.float32
    )
    attn_latent = mixed.astype(jnp.bfloat16)
    by_target = attn_latent.reshape(requests, steps_count, 32, 4, LAT)
    by_target = jnp.transpose(by_target, (2, 3, 1, 0, 4)).reshape(32, 32, LAT)
    head_rows = lax.all_to_all(by_target, "ep", split_axis=0, concat_axis=0, tiled=True)
    operands = layer_operands(resid, routes, w_out, norm_gain, router_w, w_gate, w_up, w_down)
    halves = layer_call(head_rows, w_uv, *operands)
    rows = jnp.swapaxes(halves, 0, 1).astype(jnp.bfloat16)
    return rows.reshape(steps_count, requests, 2 * HALF)


def solution(mesh):
    placed = (
        P("ctx", "ep", None, None, None),
        P("ctx", "ep", None, None),
        P(("ctx", "ep")),
        P(None, ("ctx", "ep"), None),
        P(None, ("ctx", "ep"), None),
        P(None, ("ctx", "ep"), None),
        P("ep", None, None),
        P("ep", None),
        P(),
        P(),
        P(None, ("ctx", "ep"), None),
        P("ep", None, "ctx"),
        P("ep", None, "ctx"),
        P("ep", "ctx", None),
    )
    return jax.shard_map(
        per_device,
        mesh=mesh,
        in_specs=placed,
        out_specs=P(None, ("ctx", "ep"), None),
        check_vma=False,
    )
```

time: 520 us -> 311 us (0.60)
  waiting for transfers between devices: 238 us -> 91.1 us
  Pallas kernels: 0 us -> 142 us
  blocking collectives: 122 us -> 0 us
  matrix products: 42.8 us -> 10.3 us
  local copies, waits for them, and re-layouts: 77 us -> 48.4 us
  between operations: 14 us -> 0.21 us
  other arithmetic: 9.92 us -> 3.87 us
    pallas_call x0 -> x1, Pallas kernels: none -> 142 us  [layer_call(): pl.pallas_call(layer_kernel, out_shape=jax.ShapeDtypeStruct((2, 8, HALF),...]
    all_to_all x2 -> x0, blocking collectives: 122 us -> none  [the longest x1 96.1 us: per_device(): lax.all_to_all(spread, ('ctx', 'ep'), split_axis=0, concat_axis=0, tiled=...]
    reduce_scatter x1 -> x0, waiting for transfers between devices: 74.6 us -> none  [per_device(): lax.psum_scatter(jnp.dot(flat_heads, w_out, preferred_element_type=jnp.fl...]
    all_to_all x1, waiting for transfers between devices: 85.1 us -> 12.4 us  [per_device(): lax.all_to_all(by_target, 'ep', split_axis=0, concat_axis=0, tiled=True)]
    dot_general x7 -> x0, matrix products: 32.5 us -> none  [the longest x1 16 us: expert_ffn(): jnp.dot(hidden_units, w_down[0], preferred_element_type=jnp.float32)]
    reshape x3, local copies, waits for them, and re-layouts: 25.8 us -> 2.67 us  [the longest x1 1.13 us: per_device(): by_target = jnp.transpose(by_target, (2, 3, 1, 0, 4)).reshape(32, 32, LAT)]
    reduce_sum x4 -> x0, other arithmetic: 7.88 us -> none  [the longest x1 7.49 us: per_device(): expert_out = jnp.sum(shard_terms, axis=0).astype(jnp.bfloat16)]
    broadcast_in_dim x1 -> x0, local copies, waits for them, and re-layouts: 5.27 us -> none  [per_device(): jnp.broadcast_to(send[None], (ctx_count,) + send.shape)]
  transfers between devices with their start and end apart: 3 -> 2, of which waited for: 3 -> 2; matrix products, arithmetic and copies ran while one was open for 1% -> 2% of each run, Pallas kernels for 0% -> 0%
where the time goes in v1:
time: 311 us; the launch traced here: 310 us
  Pallas kernels  142 us (46%)
  waiting for transfers between devices  91.1 us (29%)
  local copies, waits for them, and re-layouts  48.4 us (16%)
  starting transfers between devices  14.5 us (5%)
  matrix products  10.3 us (3%)
  other arithmetic  3.87 us (1%)
    pallas_call x1, Pallas kernels, layer_call(): pl.pallas_call(layer_kernel, out_shape=jax.ShapeDtypeStruct((2, 8, HALF),...  142 us
    all_to_all x1, waiting for transfers between devices, per_device(): lax.all_to_all(prefill_pages, 'ctx', split_axis=2, concat_axis=0, tiled=T...  78.7 us
    scatter x1, local copies, waits for them, and re-layouts, per_device(): placed = jnp.zeros_like(stacked).at[targets].set(stacked)  13.4 us
    all_to_all x1, waiting for transfers between devices, per_device(): lax.all_to_all(by_target, 'ep', split_axis=0, concat_axis=0, tiled=True)  12.4 us
    reshape x1, local copies, waits for them, and re-layouts, per_device(): page_cache = placed.reshape(requests, -1, LATW)  12 us
    unnamed x22, local copies, waits for them, and re-layouts  10.9 us
    all_to_all x1, starting transfers between devices, per_device(): lax.all_to_all(by_target, 'ep', split_axis=0, concat_axis=0, tiled=True)  8.47 us
  transfers between devices with their start and end apart: 2, of which 2 were waited for; matrix products, arithmetic and copies ran while one was open for 2% of the time, Pallas kernels for 0%

profile of v1, /device:TPU:1, one launch (start us, length us, event | category | flops | bytes accessed | tf_op | source)
XLA Modules:
  0.0 310.3 jit_solution(16311417070398010383)
XLA Ops:
  0.0 8.9 %copy.45 = bf16[1,1,4,20,36864]{4,3,1,0,2:T(8,128)(2,1)} copy(bf16[1,1,4,20,36864]{4,2,3,1,0:T(4,128)(2,1)} %param.14) | data formatting | bytes 11796480 | tf_op args[0]
  8.9 0.0 copy-start.8
  8.9 0.0 copy-start.1
  8.9 0.0 copy-start.6
  8.9 0.0 copy-start.9
  8.9 6.0 %all-to-all-start = ((bf16[1,1,4,20,36864]{4,3,1,0,2:T(8,128)(2,1)}), bf16[1,1,4,20,36864]{4,3,1,0,2:T(8,128)(2,1)}, u32[]{:S(2)}, u32[]{:S(2)}) async-start(bf16[1,1,4,20,36864]{4,3,1,0,2:T(8,128)(2,1)} %copy.45), calls=%async_computation | async-start | bytes 14155776 | tf_op jit(solution)/shard_map/all_to_all | solution.py:501
  14.9 0.0 copy-done.8
  14.9 0.1 reshape.108
  15.0 0.0 copy-done.1
  15.0 1.3 reshape.111
  16.4 0.0 copy-done.6
  16.4 0.5 fusion.29
  16.9 0.0 copy-done.9
  16.9 0.1 iota_compare_fusion.1
  17.0 78.7 %all-to-all-done = bf16[1,1,4,20,36864]{4,3,1,0,2:T(8,128)(2,1)} async-done(((bf16[1,1,4,20,36864]{4,3,1,0,2:T(8,128)(2,1)}), bf16[1,1,4,20,36864]{4,3,1,0,2:T(8,128)(2,1)}, u32[]{:S(2)}, u32[]{:S(2)}) %all-to-all-start) | async-done | bytes 5898272 | tf_op jit(solution)/shard_map/all_to_all | solution.py:501
  95.6 5.4 %reshape.126 = bf16[80,36864]{1,0:T(8,128)(2,1)} reshape(bf16[1,1,4,20,36864]{4,3,1,0,2:T(8,128)(2,1)} %all-to-all-done) | data formatting | bytes 11796480 | tf_op jit(solution)/shard_map/reshape | solution.py:503
  101.0 13.4 %scatter_custom_fusion = bf16[80,36864]{1,0:T(8,128)(2,1)} fusion(s32[80]{0:T(128)S(1)} %fusion.26, bf16[80,36864]{1,0:T(8,128)(2,1)} %reshape.126, bf16[]{:T(256)} %constant.8.clone.1), kind=kCustom, calls=%fused_computation.11 | custom fusion | bytes 5898752 | tf_op jit(solution)/shard_map/scatter | solution.py:506
  114.4 12.0 %reshape.110 = bf16[4,1280,576]{2,1,0:T(8,128)(2,1)} reshape(bf16[80,36864]{1,0:T(8,128)(2,1)} %scatter_custom_fusion) | data formatting | bytes 11796480 | tf_op jit(solution)/shard_map/reshape | solution.py:507
  126.5 0.0 copy-start
  126.5 5.6 %bitcast_reduce_fusion = (f32[4,2,128]{2,1,0:T(2,128)S(1)}, f32[4,1280,2,128]{3,1,2,0:T(8,128)S(1)}) fusion(pred[4,1280]{1,0:T(4,128)(4,1)S(1)} %iota_compare_fusion.1, bf16[2,4,128,576]{3,2,1,0:T(8,128)(2,1)S(1)} %reshape.111, bf16[4,1280,576]{2,1,0:T(8,128)(2,1)} %reshape.110), kind=kOutput, calls=%fused_computation.6 | convolution fusion | flops 1513880576 | bytes 12329984 | tf_op jit(solution)/shard_map/sqhd,qld->qshl/dot_general | solution.py:513
  132.1 1.5 fusion.4
  133.6 0.0 copy-done
  133.6 3.7 %fusion.2 = f32[4,2,128,512]{3,2,1,0:T(8,128)S(1)} fusion(bf16[4,1280,576]{2,1,0:T(8,128)(2,1)S(1)} %copy-done, f32[4,1280,2,128]{3,1,2,0:T(8,128)S(1)} %get-tuple-element.6, f32[4,2,128]{2,1,0:T(2,128)S(1)} %add.28, f32[4,2,128]{2,1,0:T(2,128)S(1)} %max.7, pred[4,1280]{1,0:T(4,128)(4,1)S(1)} %iota_compare_fusion.1), kind=kOutput, calls=%fused_computation.4 | convolution fusion | flops 1348730880 | bytes 12596224 | tf_op jit(solution)/shard_map/qshl,qlc->qshc/dot_general | solution.py:530
  137.4 0.0 copy-start.4
  137.4 0.0 copy-start.7
  137.4 0.0 copy-start.5
  137.4 0.0 copy-start.3
  137.4 0.5 add_convert_fusion
  137.9 0.8 copy.69
  138.7 1.1 reshape.113
  139.9 8.5 %all-to-all-start.1 = ((bf16[32,32,512]{2,1,0:T(8,128)(2,1)}), bf16[32,32,512]{2,1,0:T(8,128)(2,1)S(1)}, u32[]{:S(2)}, u32[]{:S(2)}) async-start(bf16[32,32,512]{2,1,0:T(8,128)(2,1)} %reshape.113), calls=%async_computation.1 | async-start | bytes 2097152 | tf_op jit(solution)/shard_map/all_to_all | solution.py:539
  148.4 0.0 copy-done.4
  148.4 0.2 reshape.121
  148.5 0.7 copy.91
  149.3 0.0 copy-done.7
  149.3 0.1 fusion.21
  149.4 0.6 convert_element_type.34.chosen_ref
  150.0 0.0 copy-done.5
  150.0 0.6 reshape.119
  150.6 0.0 copy-done.3
  150.6 0.9 copy.71
  151.5 1.6 pad.4.clone
  153.1 12.4 %all-to-all-done.1.heads_ref = bf16[32,32,512]{2,1,0:T(8,128)(2,1)S(1)} async-done(((bf16[32,32,512]{2,1,0:T(8,128)(2,1)}), bf16[32,32,512]{2,1,0:T(8,128)(2,1)S(1)}, u32[]{:S(2)}, u32[]{:S(2)}) %all-to-all-start.1) | async-done | bytes 1048608 | tf_op jit(solution)/shard_map/all_to_all | solution.py:539
  165.5 1.0 copy-done.2
  166.5 142.0 %layer.1 = f32[2,8,3584]{2,1,0:T(8,128)} custom-call(bf16[32,32,512]{2,1,0:T(8,128)(2,1)} %copy-done.2, bf16[4,512,128]{2,1,0:T(8,128)(2,1)} %w_uv_ref.1, f32[2,8,3584]{2,1,0:T(8,128)} %bitcast.49, f32[8,128]{1,0:T(8,128)} %convert_element_type.34.chosen_ref, f32[2,1,3584]{2,1,0:T(1,128)} %bitcast.50, bf16[2,3584,128]{2,1,0:T(8,128)(2,1)} %bitcast.48, ...), custom_call_target="tpu_custom_call" | custom-call | flops 20000000000 | bytes 22000000 | tf_op jit(solution)/shard_map/layer/pallas_call | solution.py:451
  308.5 1.0 convert_bitcast_fusion
  309.5 0.1 copy.55
  309.6 0.7 reshape.118
  (7 shorter events, 0.1 us)
Async XLA Ops:
  8.9 6.0 %copy-start.8 = (s32[1,1,4,20]{3,2,1,0:T(4,128)S(1)}, s32[1,1,4,20]{3,2,1,0:T(4,128)}, u32[]{:S(2)}) copy-start(s32[1,1,4,20]{3,2,1,0:T(4,128)} %param.15) | copy-start | bytes 964
  8.9 6.1 %copy-start.1 = (bf16[2,4,73728]{2,1,0:T(4,128)(2,1)S(1)}, bf16[2,4,73728]{2,1,0:T(4,128)(2,1)}, u32[]{:S(2)}) copy-start(bf16[2,4,73728]{2,1,0:T(4,128)(2,1)} %param.17) | copy-start | bytes 3538948
  8.9 7.4 %copy-start.6 = (bf16[2,4,576]{2,1,0:T(4,128)(2,1)S(1)}, bf16[2,4,576]{2,1,0:T(4,128)(2,1)}, u32[]{:S(2)}) copy-start(bf16[2,4,576]{2,1,0:T(4,128)(2,1)} %param.18) | copy-start | bytes 27652
  8.9 8.0 %copy-start.9 = (s32[4]{0:T(128)S(1)}, s32[4]{0:T(128)}, u32[]{:S(2)}) copy-start(s32[4]{0:T(128)} %param.16) | copy-start | bytes 52
  8.9 86.7 %all-to-all-start = ((bf16[1,1,4,20,36864]{4,3,1,0,2:T(8,128)(2,1)}), bf16[1,1,4,20,36864]{4,3,1,0,2:T(8,128)(2,1)}, u32[]{:S(2)}, u32[]{:S(2)}) async-start(bf16[1,1,4,20,36864]{4,3,1,0,2:T(8,128)(2,1)} %copy.45), calls=%async_computation | async-start | bytes 14155776 | tf_op jit(solution)/shard_map/all_to_all | solution.py:501
  126.5 7.2 %copy-start = (bf16[4,1280,576]{2,1,0:T(8,128)(2,1)S(1)}, bf16[4,1280,576]{2,1,0:T(8,128)(2,1)}, u32[]{:S(2)}) copy-start(bf16[4,1280,576]{2,1,0:T(8,128)(2,1)} %reshape.110) | copy-start | bytes 17694724
  137.4 11.0 %copy-start.4 = (bf16[2,4,7168]{2,1,0:T(4,128)(2,1)S(1)}, bf16[2,4,7168]{2,1,0:T(4,128)(2,1)}, u32[]{:S(2)}) copy-start(bf16[2,4,7168]{2,1,0:T(4,128)(2,1)} %param.19) | copy-start | bytes 344068
  137.4 11.9 %copy-start.7 = (s32[2,4,8]{2,1,0:T(4,128)S(1)}, s32[2,4,8]{2,1,0:T(4,128)}, u32[]{:S(2)}) copy-start(s32[2,4,8]{2,1,0:T(4,128)} %param.24) | copy-start | bytes 772
  137.4 12.6 %copy-start.5 = (bf16[7168]{0:T(1024)(128)(2,1)S(1)}, bf16[7168]{0:T(1024)(128)(2,1)}, u32[]{:S(2)}) copy-start(bf16[7168]{0:T(1024)(128)(2,1)} %param.22) | copy-start | bytes 43012
  137.4 13.2 %copy-start.3 = (bf16[7168,32]{0,1:T(8,128)(2,1)S(1)}, bf16[7168,32]{0,1:T(8,128)(2,1)}, u32[]{:S(2)}) copy-start(bf16[7168,32]{0,1:T(8,128)(2,1)} %param.23) | copy-start | bytes 1376260
  139.9 25.7 %all-to-all-start.1 = ((bf16[32,32,512]{2,1,0:T(8,128)(2,1)}), bf16[32,32,512]{2,1,0:T(8,128)(2,1)S(1)}, u32[]{:S(2)}, u32[]{:S(2)}) async-start(bf16[32,32,512]{2,1,0:T(8,128)(2,1)} %reshape.113), calls=%async_computation.1 | async-start | bytes 2097152 | tf_op jit(solution)/shard_map/all_to_all | solution.py:539
  165.5 1.0 copy-start.2

commit v2 on v1

--- a/solution.py
+++ b/solution.py
@@ -482,6 +482,309 @@
     )
 
 
+CHUNKS = 8
+CHUNK = 4608
+PAIR = 2 * LATW
+WIDE = 640
+AHEAD = 3
+
+
+def attend_kernel(
+    length_ref,
+    pages_hbm,
+    perm_ref,
+    query_ref,
+    fresh_ref,
+    heads_ref,
+    pages,
+    passing,
+    rows32,
+    query_even,
+    query_odd,
+    keys,
+    acc_even,
+    acc_odd,
+    row_max,
+    row_sum,
+    out32,
+    out16,
+    own_sem,
+    link_send,
+    link_recv,
+    head_send,
+    head_recv,
+):
+    f32, bf16 = jnp.float32, jnp.bfloat16
+    z, ep = lax.axis_index("ctx"), lax.axis_index("ep")
+    above, below, far = lax.rem(z + 1, 4), lax.rem(z + 3, 4), lax.rem(z + 2, 4)
+    up, down = (above, ep), (below, ep)
+
+    def lanes(j):
+        return pl.ds(pl.multiple_of(j * CHUNK, 128), CHUNK)
+
+    def half(j, k):
+        return pl.ds(pl.multiple_of(j * CHUNK + k * (CHUNK // 2), 128), CHUNK // 2)
+
+    def copy(kind, j, src, dst, device):
+        return pltpu.make_async_remote_copy(
+            src_ref=src,
+            dst_ref=dst,
+            send_sem=link_send.at[kind, j],
+            recv_sem=link_recv.at[kind, j],
+            device_id=device,
+            device_id_type=MESH_IDS,
+        )
+
+    def outgoing(kind, j):
+        if kind == 0:
+            return copy(0, j, pages_hbm.at[far, :, half(j, 0)], passing.at[:, half(j, 0)], up)
+        if kind == 1:
+            return copy(1, j, pages_hbm.at[far, :, half(j, 1)], passing.at[:, half(j, 1)], down)
+        if kind == 2:
+            return copy(2, j, pages_hbm.at[above, :, lanes(j)], pages.at[z, :, lanes(j)], up)
+        if kind == 3:
+            return copy(3, j, pages_hbm.at[below, :, lanes(j)], pages.at[z, :, lanes(j)], down)
+        if kind == 4:
+            return copy(4, j, passing.at[:, half(j, 0)], pages.at[below, :, half(j, 0)], up)
+        return copy(5, j, passing.at[:, half(j, 1)], pages.at[above, :, half(j, 1)], down)
+
+    def arrived(kind, j):
+        place = (
+            passing.at[:, half(j, 0)],
+            passing.at[:, half(j, 1)],
+            pages.at[below, :, lanes(j)],
+            pages.at[above, :, lanes(j)],
+            pages.at[far, :, half(j, 0)],
+            pages.at[far, :, half(j, 1)],
+        )[kind]
+        copy(kind, j, place, place, up).wait_recv()
+
+    def own(j):
+        return pltpu.make_async_copy(
+            pages_hbm.at[z, :, lanes(j)], pages.at[z, :, lanes(j)], own_sem.at[j]
+        )
+
+    def issue(j):
+        for kind in range(4):
+            outgoing(kind, j).start()
+
+    def forward(j):
+        for kind in (0, 1):
+            arrived(kind, j)
+            outgoing(kind + 4, j).start()
+
+    barrier = pltpu.get_barrier_semaphore()
+    for device in (up, down):
+        pl.semaphore_signal(barrier, inc=1, device_id=device, device_id_type=MESH_IDS)
+
+    @pl.loop(1, 32)
+    def _(d):
+        device = (z, lax.rem(ep + d, 32))
+        pl.semaphore_signal(barrier, inc=1, device_id=device, device_id_type=MESH_IDS)
+
+    pl.semaphore_wait(barrier, 33)
+
+    for j in range(AHEAD):
+        issue(j)
+
+    @pl.loop(0, CHUNKS)
+    def _(j):
+        own(j).start()
+
+    forward(0)
+
+    @pl.loop(0, 64)
+    def _(pair):
+        span = pl.ds(pl.multiple_of(pair * PAIR, 128), PAIR)
+        both = [query_ref[s, :, span].astype(f32) for s in range(2)]
+        both = jnp.concatenate(both, axis=0)
+        for k in range(PAIR // 128):
+            rows32[k, pl.ds(pl.multiple_of(pair * 8, 8), 8), :] = both[:, k * 128 : k * 128 + 128]
+
+    lane = lax.broadcasted_iota(jnp.int32, (64, WIDE), 1)
+    for q in range(4):
+        for s in range(2):
+            rows = jnp.concatenate(
+                [rows32[k, pl.ds(s * 4 + q, 64, stride=8), :] for k in range(PAIR // 128)], axis=1
+            )
+            even = jnp.where(lane < LATW, rows[:, :WIDE], 0.0)
+            odd = jnp.where(lane >= 64, rows[:, PAIR - WIDE :], 0.0)
+            for parity, value, shift in ((0, even, 64), (1, odd, WIDE - 64)):
+                place = pl.ds(s * 128 + parity * 64, 64)
+                moved = pltpu.roll(value, shift, axis=1).astype(bf16)
+                value = value.astype(bf16)
+                query_even[q, place, :] = value if parity == 0 else moved
+                query_odd[q, place, :] = moved if parity == 0 else value
+
+    scale = (NOPE + ROPE) ** (-0.5)
+    contract = (((1,), (1,)), ((), ()))
+
+    @pl.loop(0, 4)
+    def _(q):
+        fresh = fresh_ref[q]
+        score = (
+            lax.dot_general(query_even[q], fresh, contract, preferred_element_type=f32) * scale
+        )
+        token = lax.broadcasted_iota(jnp.int32, (256, 128), 1)
+        step = lax.broadcasted_iota(jnp.int32, (256, 128), 0) // 128
+        score = jnp.where(token <= step, score, masked_score)
+        top = jnp.max(score, axis=1, keepdims=True)
+        weight = jnp.exp(score - top)
+        row_max[q] = jnp.broadcast_to(top, (256, 128))
+        row_sum[q] = jnp.broadcast_to(jnp.sum(weight, axis=1, keepdims=True), (256, 128))
+        acc_even[q] = jnp.dot(weight.astype(bf16), fresh[:, :LAT], preferred_element_type=f32)
+        acc_odd[q] = jnp.zeros((256, WIDE), f32)
+
+    @pl.loop(0, CHUNKS)
+    def _(j):
+        @pl.when(j + AHEAD < CHUNKS)
+        def _():
+            issue(j + AHEAD)
+
+        @pl.when(j + 1 < CHUNKS)
+        def _():
+            forward(j + 1)
+
+        own(j).wait()
+        for kind in (2, 3, 4, 5):
+            arrived(kind, j)
+
+        for i in range(4):
+            span = pl.ds(pl.multiple_of(j * CHUNK + i * PAIR, 128), PAIR)
+            found = [
+                jnp.dot(perm_ref[c], pages[c, :, span], preferred_element_type=f32)
+                for c in range(4)
+            ]
+            for q in range(4):
+                rows = jnp.concatenate([one[q * 8 : q * 8 + 8] for one in found], axis=0)
+                keys[q, pl.ds(i * 32, 32), :] = rows.astype(bf16)
+
+        @pl.loop(0, 4)
+        def _(q):
+            key = keys[q]
+            low, high = key[:, :WIDE], key[:, PAIR - WIDE :]
+            score = jnp.concatenate(
+                [
+                    lax.dot_general(query_even[q], low, contract, preferred_element_type=f32),
+                    lax.dot_general(query_odd[q], high, contract, preferred_element_type=f32),
+                ],
+                axis=1,
+            )
+            n = lax.broadcasted_iota(jnp.int32, (1, 256), 1)
+            fifth = n % 8
+            page = 4 * fifth + (n % 32) // 8
+            position = page * 64 + 2 * (4 * j + (n % 128) // 32) + n // 128
+            live = (fifth < 5) & (position < length_ref[q])
+            score = jnp.where(live, score * scale, masked_score)
+            before = row_max[q]
+            top = jnp.maximum(before, jnp.max(score, axis=1, keepdims=True))
+            shrink = jnp.exp(before - top)
+            weight = jnp.exp(score - jnp.concatenate([top, top], axis=1))
+            row_max[q] = top
+            row_sum[q] = row_sum[q] * shrink + jnp.sum(weight, axis=1, keepdims=True)
+            weight = weight.astype(bf16)
+            acc_even[q] = acc_even[q] * shrink[:, :1] + jnp.dot(
+                weight[:, :128], low[:, :LAT], preferred_element_type=f32
+            )
+            acc_odd[q] = acc_odd[q] * shrink[:, :1] + jnp.dot(
+                weight[:, 128:], high, preferred_element_type=f32
+            )
+
+    for q in range(4):
+        value = (acc_even[q] + acc_odd[q][:, 64 : 64 + LAT]) / row_sum[q][:, :1]
+        for block in range(4):
+            s, parity = block // 2, block % 2
+            for k in range(LAT // 128):
+                out32[k, pl.ds(parity * 8 + s * 4 + q, 64, stride=16), :] = value[
+                    block * 64 : block * 64 + 64, k * 128 : k * 128 + 128
+                ]
+
+    @pl.loop(0, 32)
+    def _(e):
+        for k in range(LAT // 128):
+            out16[e, :, pl.ds(k * 128, 128)] = out32[
+                k, pl.ds(pl.multiple_of(e * 32, 32), 32), :
+            ].astype(bf16)
+
+    def head_copy(d, src, dst, device):
+        return pltpu.make_async_remote_copy(
+            src_ref=src,
+            dst_ref=dst,
+            send_sem=head_send.at[d],
+            recv_sem=head_recv.at[d],
+            device_id=device,
+            device_id_type=MESH_IDS,
+        )
+
+    def head_block(d):
+        target = lax.rem(ep + d, 32)
+        return head_copy(d, out16.at[target], heads_ref.at[ep], (z, target))
+
+    @pl.loop(1, 32)
+    def _(d):
+        head_block(d).start()
+
+    heads_ref[ep] = out16[ep]
+
+    @pl.loop(1, 32)
+    def _(d):
+        source = heads_ref.at[lax.rem(ep + 32 - d, 32)]
+        head_copy(d, source, source, up).wait_recv()
+
+    @pl.loop(1, 32)
+    def _(d):
+        head_block(d).wait_send()
+
+    @pl.loop(0, CHUNKS)
+    def _(j):
+        for kind in range(6):
+            outgoing(kind, j).wait_send()
+
+
+def attend_call(prefill_pages, page_map, prompt_len, queries, new_latent):
+    bf16, f32 = jnp.bfloat16, jnp.float32
+    slots, width = prefill_pages.shape[3:]
+    row = jnp.arange(32)
+    request, fifth = row // 8, row % 8
+    wanted = request[None, :] * 20 + 4 * fifth[None, :] + jnp.arange(4)[:, None]
+    wanted = jnp.where(fifth[None, :] < 5, wanted, -1)
+    perm = (page_map.reshape(4, 1, slots) == wanted[:, :, None]).astype(bf16)
+    fresh = jnp.pad(jnp.swapaxes(new_latent, 0, 1), ((0, 0), (0, 126), (0, WIDE - LATW)))
+    vmem, hbm = pl.BlockSpec(memory_space=pltpu.VMEM), pl.BlockSpec(memory_space=pl.ANY)
+    return pl.pallas_call(
+        attend_kernel,
+        out_shape=jax.ShapeDtypeStruct((32, 32, LAT), bf16),
+        in_specs=[pl.BlockSpec(memory_space=pltpu.SMEM), hbm, vmem, vmem, vmem],
+        out_specs=vmem,
+        scratch_shapes=[
+            pltpu.VMEM((4, slots, width), bf16),
+            pltpu.VMEM((slots, width), bf16),
+            pltpu.VMEM((PAIR // 128, 512, 128), f32),
+            pltpu.VMEM((4, 256, WIDE), bf16),
+            pltpu.VMEM((4, 256, WIDE), bf16),
+            pltpu.VMEM((4, 128, PAIR), bf16),
+            pltpu.VMEM((4, 256, LAT), f32),
+            pltpu.VMEM((4, 256, WIDE), f32),
+            pltpu.VMEM((4, 256, 128), f32),
+            pltpu.VMEM((4, 256, 128), f32),
+            pltpu.VMEM((LAT // 128, 1024, 128), f32),
+            pltpu.VMEM((32, 32, LAT), bf16),
+            pltpu.SemaphoreType.DMA((CHUNKS,)),
+            pltpu.SemaphoreType.DMA((6, CHUNKS)),
+            pltpu.SemaphoreType.DMA((6, CHUNKS)),
+            pltpu.SemaphoreType.DMA((32,)),
+            pltpu.SemaphoreType.DMA((32,)),
+        ],
+        compiler_params=pltpu.CompilerParams(
+            collective_id=2, has_side_effects=True, vmem_limit_bytes=56 * 1024 * 1024
+        ),
+        cost_estimate=pl.CostEstimate(
+            flops=4_000_000_000, bytes_accessed=8_000_000, transcendentals=1_500_000
+        ),
+        name="attend",
+    )(prompt_len, prefill_pages.reshape(4, slots, width), perm, queries, fresh)
+
+
 def per_device(
     prefill_pages,
     page_map,
@@ -498,49 +801,11 @@
     w_up,
     w_down,
 ):
-    received = lax.all_to_all(prefill_pages, "ctx", split_axis=2, concat_axis=0, tiled=True)
-    page_width = received.shape[-1]
-    stacked = received.reshape(-1, page_width)
-    targets = page_map.reshape(-1)
-    requests = prompt_len.shape[0]
-    placed = jnp.zeros_like(stacked).at[targets].set(stacked)
-    page_cache = placed.reshape(requests, -1, LATW)
-    key_count = page_cache.shape[1]
-    steps_count = queries.shape[0]
-    query_rows = queries.reshape(steps_count, requests, -1, LATW)
-    score_scale = (NOPE + ROPE) ** (-0.5)
-    old_scores = (
-        jnp.einsum("sqhd,qld->qshl", query_rows, page_cache, preferred_element_type=jnp.float32)
-        * score_scale
-    )
-    new_scores = (
-        jnp.einsum("sqhd,jqd->qshj", query_rows, new_latent, preferred_element_type=jnp.float32)
-        * score_scale
-    )
-    live_keys = jnp.arange(key_count)[None, :] < prompt_len[:, None]
-    old_scores = jnp.where(live_keys[:, None, None, :], old_scores, masked_score)
-    causal = jnp.arange(steps_count)[None, :] <= jnp.arange(steps_count)[:, None]
-    new_scores = jnp.where(causal[None, :, None, :], new_scores, masked_score)
-    row_max = jnp.maximum(old_scores.max(-1), new_scores.max(-1))[..., None]
-    old_exp = jnp.exp(old_scores - row_max)
-    new_exp = jnp.exp(new_scores - row_max)
-    row_total = old_exp.sum(-1, keepdims=True) + new_exp.sum(-1, keepdims=True)
-    old_weights = (old_exp / row_total).astype(jnp.bfloat16)
-    new_weights = (new_exp / row_total).astype(jnp.bfloat16)
-    mixed = jnp.einsum(
-        "qshl,qlc->qshc", old_weights, page_cache[:, :, :LAT], preferred_element_type=jnp.float32
-    )
-    mixed = mixed + jnp.einsum(
-        "qshj,jqc->qshc", new_weights, new_latent[:, :, :LAT], preferred_element_type=jnp.float32
-    )
-    attn_latent = mixed.astype(jnp.bfloat16)
-    by_target = attn_latent.reshape(requests, steps_count, 32, 4, LAT)
-    by_target = jnp.transpose(by_target, (2, 3, 1, 0, 4)).reshape(32, 32, LAT)
-    head_rows = lax.all_to_all(by_target, "ep", split_axis=0, concat_axis=0, tiled=True)
+    head_rows = attend_call(prefill_pages, page_map, prompt_len, queries, new_latent)
     operands = layer_operands(resid, routes, w_out, norm_gain, router_w, w_gate, w_up, w_down)
     halves = layer_call(head_rows, w_uv, *operands)
     rows = jnp.swapaxes(halves, 0, 1).astype(jnp.bfloat16)
-    return rows.reshape(steps_count, requests, 2 * HALF)
+    return rows.reshape(resid.shape)
 
 
 def solution(mesh):

time: 311 us -> 276 us (0.89)
  Pallas kernels: 142 us -> 259 us
  waiting for transfers between devices: 91.1 us -> 0 us
  local copies, waits for them, and re-layouts: 48.4 us -> 14.2 us
  starting transfers between devices: 14.5 us -> 0 us
  matrix products: 10.3 us -> 0 us
    pallas_call x0 -> x1, Pallas kernels: none -> 115 us  [attend_call(): pl.pallas_call(attend_kernel, out_shape=jax.ShapeDtypeStruct((32, 32, LAT...]
    all_to_all x2 -> x0, waiting for transfers between devices: 91.1 us -> none  [the longest x1 78.7 us: per_device(): lax.all_to_all(prefill_pages, 'ctx', split_axis=2, concat_axis=0, tiled=T...]
    reshape x7 -> x1, local copies, waits for them, and re-layouts: 21.5 us -> 0.72 us  [per_device(): return rows.reshape(resid.shape)]
    all_to_all x2 -> x0, starting transfers between devices: 14.5 us -> none  [the longest x1 8.47 us: per_device(): lax.all_to_all(by_target, 'ep', split_axis=0, concat_axis=0, tiled=True)]
    scatter x1 -> x0, local copies, waits for them, and re-layouts: 13.4 us -> none  [per_device(): placed = jnp.zeros_like(stacked).at[targets].set(stacked)]
    dot_general x4 -> x0, matrix products: 10.3 us -> none  [the longest x1 5.6 us: per_device(): jnp.einsum('sqhd,qld->qshl', query_rows, page_cache, preferred_element_ty...]
    unnamed x22 -> x15, local copies, waits for them, and re-layouts: 10.9 us -> 9.88 us
  transfers between devices with their start and end apart: 2 -> 0, of which waited for: 2 -> 0; matrix products, arithmetic and copies ran while one was open for 2% -> 0% of each run, Pallas kernels for 0% -> 0%
where the time goes in v2:
time: 276 us
  Pallas kernels  259 us (94%)
  local copies, waits for them, and re-layouts  14.2 us (5%)
  other arithmetic  2.98 us (1%)
    pallas_call x1, Pallas kernels, layer_call(): pl.pallas_call(layer_kernel, out_shape=jax.ShapeDtypeStruct((2, 8, HALF),...  144 us
    pallas_call x1, Pallas kernels, attend_call(): pl.pallas_call(attend_kernel, out_shape=jax.ShapeDtypeStruct((32, 32, LAT...  115 us
    unnamed x15, local copies, waits for them, and re-layouts  9.88 us

profile of v2, /device:TPU:1, one launch (start us, length us, event | category | flops | bytes accessed | tf_op | source)
XLA Modules:
  0.0 275.8 jit_solution(14934683891489871380)
XLA Ops:
  0.0 0.0 copy-start.3
  0.0 0.0 copy-start.5
  0.0 8.9 %copy.32 = bf16[1,1,4,20,36864]{4,3,2,1,0:T(8,128)(2,1)} copy(bf16[1,1,4,20,36864]{4,2,3,1,0:T(4,128)(2,1)} %param.14) | data formatting | bytes 11796480 | tf_op args[0]
  8.9 0.0 copy-done.3
  8.9 1.0 pad.8.fresh_ref
  9.9 0.0 copy-done.5
  9.9 0.7 compare_convert_fusion.perm_ref
  10.6 0.0 copy-start
  10.6 114.5 %attend.1.heads_ref = bf16[32,32,512]{2,1,0:T(8,128)(2,1)} custom-call(s32[4]{0:T(128)} %length_ref.1, bf16[4,20,36864]{2,1,0:T(8,128)(2,1)} %bitcast.19, bf16[4,32,20]{2,1,0:T(8,128)(2,1)} %compare_convert_fusion.perm_ref, bf16[2,4,73728]{2,1,0:T(4,128)(2,1)} %query_ref.1, bf16[4,128,640]{2,1,0:T(8,128)(2,1)} %pad.8.fresh_ref), custom_call_target="tpu_custom_call" | custom-call | flops 4000000000 | bytes 8000000 | tf_op jit(solution)/shard_map/attend/pallas_call | solution.py:754
  125.2 0.0 copy-done
  125.2 0.0 copy-start.1
  125.2 0.0 copy-start.2
  125.2 0.0 copy-start.4
  125.2 0.9 copy.28
  126.2 1.6 pad.9.clone
  127.8 0.0 copy-done.1
  127.8 0.1 reshape.94
  128.0 0.7 copy.33
  128.7 0.0 copy-done.2
  128.7 0.6 reshape.92
  129.3 0.0 copy-done.4
  129.3 0.1 fusion
  129.4 0.6 convert_element_type.28.chosen_ref
  130.0 144.1 %layer.1 = f32[2,8,3584]{2,1,0:T(8,128)} custom-call(bf16[32,32,512]{2,1,0:T(8,128)(2,1)} %attend.1.heads_ref, bf16[4,512,128]{2,1,0:T(8,128)(2,1)} %w_uv_ref.1, f32[2,8,3584]{2,1,0:T(8,128)} %bitcast.21, f32[8,128]{1,0:T(8,128)} %convert_element_type.28.chosen_ref, f32[2,1,3584]{2,1,0:T(1,128)} %bitcast.23, bf16[2,3584,128]{2,1,0:T(8,128)(2,1)} %bitcast.20, ...), custom_call_target="tpu_custom_call" | custom-call | flops 20000000000 | bytes 22000000 | tf_op jit(solution)/shard_map/layer/pallas_call | solution.py:451
  274.1 1.0 convert_bitcast_fusion
  275.0 0.1 copy.27
  275.1 0.7 reshape.91
  (4 shorter events, 0.0 us)
Async XLA Ops:
  0.0 8.9 %copy-start.3 = (bf16[2,4,576]{2,1,0:T(4,128)(2,1)S(1)}, bf16[2,4,576]{2,1,0:T(4,128)(2,1)}, u32[]{:S(2)}) copy-start(bf16[2,4,576]{2,1,0:T(4,128)(2,1)} %param.18) | copy-start | bytes 27652
  0.0 9.9 %copy-start.5 = (s32[1,1,4,20]{3,2,1,0:T(4,128)S(1)}, s32[1,1,4,20]{3,2,1,0:T(4,128)}, u32[]{:S(2)}) copy-start(s32[1,1,4,20]{3,2,1,0:T(4,128)} %param.15) | copy-start | bytes 964
  10.6 114.6 %copy-start = (bf16[7168,32]{0,1:T(8,128)(2,1)S(1)}, bf16[7168,32]{0,1:T(8,128)(2,1)}, u32[]{:S(2)}) copy-start(bf16[7168,32]{0,1:T(8,128)(2,1)} %param.23) | copy-start | bytes 1376260
  125.2 2.6 copy-start.1
  125.2 3.5 %copy-start.2 = (bf16[7168]{0:T(1024)(128)(2,1)S(1)}, bf16[7168]{0:T(1024)(128)(2,1)}, u32[]{:S(2)}) copy-start(bf16[7168]{0:T(1024)(128)(2,1)} %param.22) | copy-start | bytes 43012
  125.2 4.1 %copy-start.4 = (s32[2,4,8]{2,1,0:T(4,128)S(1)}, s32[2,4,8]{2,1,0:T(4,128)}, u32[]{:S(2)}) copy-start(s32[2,4,8]{2,1,0:T(4,128)} %param.24) | copy-start | bytes 772

commit v3 on v2

--- a/solution.py
+++ b/solution.py
@@ -483,10 +483,10 @@
 
 
 CHUNKS = 8
-CHUNK = 4608
 PAIR = 2 * LATW
 WIDE = 640
-AHEAD = 3
+QUARTER = 9216
+SPREAD = (2, 1, 3)
 
 
 def attend_kernel(
@@ -496,8 +496,10 @@
     query_ref,
     fresh_ref,
     heads_ref,
+    raw,
+    rows_raw,
+    packed,
     pages,
-    passing,
     rows32,
     query_even,
     query_odd,
@@ -508,6 +510,7 @@
     row_sum,
     out32,
     out16,
+    raw_sem,
     own_sem,
     link_send,
     link_recv,
@@ -516,14 +519,12 @@
 ):
     f32, bf16 = jnp.float32, jnp.bfloat16
     z, ep = lax.axis_index("ctx"), lax.axis_index("ep")
-    above, below, far = lax.rem(z + 1, 4), lax.rem(z + 3, 4), lax.rem(z + 2, 4)
-    up, down = (above, ep), (below, ep)
 
     def lanes(j):
-        return pl.ds(pl.multiple_of(j * CHUNK, 128), CHUNK)
-
-    def half(j, k):
-        return pl.ds(pl.multiple_of(j * CHUNK + k * (CHUNK // 2), 128), CHUNK // 2)
+        return pl.ds(pl.multiple_of(j * PAIR, 128), PAIR)
+
+    def ring(step):
+        return lax.rem(z + step, 4)
 
     def copy(kind, j, src, dst, device):
         return pltpu.make_async_remote_copy(
@@ -536,62 +537,68 @@
         )
 
     def outgoing(kind, j):
-        if kind == 0:
-            return copy(0, j, pages_hbm.at[far, :, half(j, 0)], passing.at[:, half(j, 0)], up)
-        if kind == 1:
-            return copy(1, j, pages_hbm.at[far, :, half(j, 1)], passing.at[:, half(j, 1)], down)
-        if kind == 2:
-            return copy(2, j, pages_hbm.at[above, :, lanes(j)], pages.at[z, :, lanes(j)], up)
-        if kind == 3:
-            return copy(3, j, pages_hbm.at[below, :, lanes(j)], pages.at[z, :, lanes(j)], down)
-        if kind == 4:
-            return copy(4, j, passing.at[:, half(j, 0)], pages.at[below, :, half(j, 0)], up)
-        return copy(5, j, passing.at[:, half(j, 1)], pages.at[above, :, half(j, 1)], down)
+        owner = ring(SPREAD[kind])
+        return copy(
+            kind, j, packed.at[owner, :, lanes(j)], pages.at[z, :, lanes(j)], (owner, ep)
+        )
 
     def arrived(kind, j):
-        place = (
-            passing.at[:, half(j, 0)],
-            passing.at[:, half(j, 1)],
-            pages.at[below, :, lanes(j)],
-            pages.at[above, :, lanes(j)],
-            pages.at[far, :, half(j, 0)],
-            pages.at[far, :, half(j, 1)],
-        )[kind]
-        copy(kind, j, place, place, up).wait_recv()
+        producer = ring(4 - SPREAD[kind])
+        place = pages.at[producer, :, lanes(j)]
+        copy(kind, j, place, place, (producer, ep)).wait_recv()
 
     def own(j):
         return pltpu.make_async_copy(
-            pages_hbm.at[z, :, lanes(j)], pages.at[z, :, lanes(j)], own_sem.at[j]
+            packed.at[z, :, lanes(j)], pages.at[z, :, lanes(j)], own_sem.at[j]
         )
 
-    def issue(j):
-        for kind in range(4):
-            outgoing(kind, j).start()
-
-    def forward(j):
-        for kind in (0, 1):
-            arrived(kind, j)
-            outgoing(kind + 4, j).start()
+    def fetch(j, quarter):
+        span = pl.ds(pl.multiple_of(quarter * QUARTER + j * PAIR, 128), PAIR)
+        return pltpu.make_async_copy(
+            pages_hbm.at[:, :, span], raw.at[:, :, span], raw_sem.at[j, quarter]
+        )
+
+    @pl.loop(0, CHUNKS)
+    def _(j):
+        for quarter in range(4):
+            fetch(j, quarter).start()
 
     barrier = pltpu.get_barrier_semaphore()
-    for device in (up, down):
-        pl.semaphore_signal(barrier, inc=1, device_id=device, device_id_type=MESH_IDS)
+    for step in SPREAD:
+        pl.semaphore_signal(barrier, inc=1, device_id=(ring(step), ep), device_id_type=MESH_IDS)
 
     @pl.loop(1, 32)
     def _(d):
         device = (z, lax.rem(ep + d, 32))
         pl.semaphore_signal(barrier, inc=1, device_id=device, device_id_type=MESH_IDS)
 
-    pl.semaphore_wait(barrier, 33)
-
-    for j in range(AHEAD):
-        issue(j)
+    pl.semaphore_wait(barrier, 34)
 
     @pl.loop(0, CHUNKS)
     def _(j):
+        for quarter in range(4):
+            fetch(j, quarter).wait()
+        for quarter in range(4):
+            span = pl.ds(pl.multiple_of(quarter * QUARTER + j * PAIR, 128), PAIR)
+
+            @pl.loop(0, 5)
+            def _(group, quarter=quarter, span=span):
+                for two in range(2):
+                    slot = group * 4 + two * 2
+                    both = jnp.concatenate(
+                        [raw[slot, :, span].astype(f32), raw[slot + 1, :, span].astype(f32)], axis=0
+                    )
+                    place = pl.ds(pl.multiple_of((group * 4 + quarter) * 16 + two * 8, 8), 8)
+                    for k in range(PAIR // 128):
+                        rows_raw[k, place, :] = both[:, k * 128 : k * 128 + 128]
+
+        for owner in range(4):
+            for k in range(PAIR // 128):
+                column = pl.ds(pl.multiple_of(j * PAIR + k * 128, 128), 128)
+                packed[owner, :, column] = rows_raw[k, pl.ds(owner, 80, stride=4), :].astype(bf16)
         own(j).start()
-
-    forward(0)
+        for kind in range(3):
+            outgoing(kind, j).start()
 
     @pl.loop(0, 64)
     def _(pair):
@@ -637,27 +644,19 @@
 
     @pl.loop(0, CHUNKS)
     def _(j):
-        @pl.when(j + AHEAD < CHUNKS)
-        def _():
-            issue(j + AHEAD)
-
-        @pl.when(j + 1 < CHUNKS)
-        def _():
-            forward(j + 1)
-
         own(j).wait()
-        for kind in (2, 3, 4, 5):
+        for kind in range(3):
             arrived(kind, j)
 
-        for i in range(4):
-            span = pl.ds(pl.multiple_of(j * CHUNK + i * PAIR, 128), PAIR)
-            found = [
-                jnp.dot(perm_ref[c], pages[c, :, span], preferred_element_type=f32)
-                for c in range(4)
-            ]
+        found = [
+            jnp.dot(perm_ref[c], pages[c, :, lanes(j)], preferred_element_type=f32)
+            for c in range(4)
+        ]
+        for quarter in range(4):
             for q in range(4):
-                rows = jnp.concatenate([one[q * 8 : q * 8 + 8] for one in found], axis=0)
-                keys[q, pl.ds(i * 32, 32), :] = rows.astype(bf16)
+                at = quarter * 32 + q * 8
+                rows = jnp.concatenate([one[at : at + 8] for one in found], axis=0)
+                keys[q, pl.ds(quarter * 32, 32), :] = rows.astype(bf16)
 
         @pl.loop(0, 4)
         def _(q):
@@ -673,7 +672,7 @@
             n = lax.broadcasted_iota(jnp.int32, (1, 256), 1)
             fifth = n % 8
             page = 4 * fifth + (n % 32) // 8
-            position = page * 64 + 2 * (4 * j + (n % 128) // 32) + n // 128
+            position = page * 64 + 2 * (8 * ((n % 128) // 32) + j) + n // 128
             live = (fifth < 5) & (position < length_ref[q])
             score = jnp.where(live, score * scale, masked_score)
             before = row_max[q]
@@ -729,7 +728,7 @@
     @pl.loop(1, 32)
     def _(d):
         source = heads_ref.at[lax.rem(ep + 32 - d, 32)]
-        head_copy(d, source, source, up).wait_recv()
+        head_copy(d, source, source, (z, ep)).wait_recv()
 
     @pl.loop(1, 32)
     def _(d):
@@ -737,7 +736,7 @@
 
     @pl.loop(0, CHUNKS)
     def _(j):
-        for kind in range(6):
+        for kind in range(3):
             outgoing(kind, j).wait_send()
 
 
@@ -748,7 +747,9 @@
     request, fifth = row // 8, row % 8
     wanted = request[None, :] * 20 + 4 * fifth[None, :] + jnp.arange(4)[:, None]
     wanted = jnp.where(fifth[None, :] < 5, wanted, -1)
-    perm = (page_map.reshape(4, 1, slots) == wanted[:, :, None]).astype(bf16)
+    slot_hit = (page_map.reshape(4, 1, 5, 1, 4) == wanted[:, :, None, None, None]).astype(bf16)
+    same = jnp.eye(4, dtype=bf16)[:, None, None, :, None]
+    perm = (slot_hit[:, None] * same).reshape(4, 128, 80)
     fresh = jnp.pad(jnp.swapaxes(new_latent, 0, 1), ((0, 0), (0, 126), (0, WIDE - LATW)))
     vmem, hbm = pl.BlockSpec(memory_space=pltpu.VMEM), pl.BlockSpec(memory_space=pl.ANY)
     return pl.pallas_call(
@@ -757,8 +758,10 @@
         in_specs=[pl.BlockSpec(memory_space=pltpu.SMEM), hbm, vmem, vmem, vmem],
         out_specs=vmem,
         scratch_shapes=[
-            pltpu.VMEM((4, slots, width), bf16),
-            pltpu.VMEM((slots, width), bf16),
+            pltpu.VMEM((slots, 4, width), bf16),
+            pltpu.VMEM((PAIR // 128, 320, 128), f32),
+            pltpu.VMEM((4, 80, QUARTER), bf16),
+            pltpu.VMEM((4, 80, QUARTER), bf16),
             pltpu.VMEM((PAIR // 128, 512, 128), f32),
             pltpu.VMEM((4, 256, WIDE), bf16),
             pltpu.VMEM((4, 256, WIDE), bf16),
@@ -769,9 +772,10 @@
             pltpu.VMEM((4, 256, 128), f32),
             pltpu.VMEM((LAT // 128, 1024, 128), f32),
             pltpu.VMEM((32, 32, LAT), bf16),
+            pltpu.SemaphoreType.DMA((CHUNKS, 4)),
             pltpu.SemaphoreType.DMA((CHUNKS,)),
-            pltpu.SemaphoreType.DMA((6, CHUNKS)),
-            pltpu.SemaphoreType.DMA((6, CHUNKS)),
+            pltpu.SemaphoreType.DMA((3, CHUNKS)),
+            pltpu.SemaphoreType.DMA((3, CHUNKS)),
             pltpu.SemaphoreType.DMA((32,)),
             pltpu.SemaphoreType.DMA((32,)),
         ],
@@ -782,7 +786,7 @@
             flops=4_000_000_000, bytes_accessed=8_000_000, transcendentals=1_500_000
         ),
         name="attend",
-    )(prompt_len, prefill_pages.reshape(4, slots, width), perm, queries, fresh)
+    )(prompt_len, jnp.swapaxes(prefill_pages[0, 0], 0, 1), perm, queries, fresh)
 
 
 def per_device(

time: 276 us -> 254 us (0.920)
  Pallas kernels: 259 us -> 244 us
  local copies, waits for them, and re-layouts: 14.2 us -> 6.92 us
    pallas_call x1, Pallas kernels: 115 us -> 100 us  [attend_call(): pl.pallas_call(attend_kernel, out_shape=jax.ShapeDtypeStruct((32, 32, LAT...]
    unnamed x15 -> x12, local copies, waits for them, and re-layouts: 9.88 us -> 1.87 us
where the time goes in v3:
time: 254 us
  Pallas kernels  244 us (96%)
  local copies, waits for them, and re-layouts  6.92 us (3%)
  other arithmetic  3.04 us (1%)
    pallas_call x1, Pallas kernels, layer_call(): pl.pallas_call(layer_kernel, out_shape=jax.ShapeDtypeStruct((2, 8, HALF),...  144 us
    pallas_call x1, Pallas kernels, attend_call(): pl.pallas_call(attend_kernel, out_shape=jax.ShapeDtypeStruct((32, 32, LAT...  100 us

profile of v3, /device:TPU:1, one launch (start us, length us, event | category | flops | bytes accessed | tf_op | source)
XLA Modules:
  0.0 254.1 jit_solution(15817699569041965573)
XLA Ops:
  0.0 0.0 copy-start.4
  0.0 0.0 copy-start.2
  0.0 1.8 copy.29
  1.9 1.6 pad.9.clone
  3.5 0.0 copy-done.4
  3.5 0.1 eq.45
  3.6 0.1 compare_convert_fusion
  3.7 0.1 mul.46
  3.8 0.2 mul.47
  4.0 0.1 copy.24
  4.1 0.1 mul.48
  4.2 0.1 mul.49
  4.3 0.1 copy.23
  4.4 0.7 broadcast_multiply_fusion.perm_ref
  5.1 0.0 copy-done.2
  5.1 0.9 pad.8.fresh_ref
  6.0 0.0 copy-start
  6.0 0.0 copy-start.1
  6.0 0.0 copy-start.3
  6.0 100.2 %attend.1.heads_ref = bf16[32,32,512]{2,1,0:T(8,128)(2,1)} custom-call(s32[4]{0:T(128)} %length_ref.1, bf16[20,4,36864]{2,1,0:T(4,128)(2,1)} %bitcast.28, bf16[4,128,80]{2,1,0:T(8,128)(2,1)} %broadcast_multiply_fusion.perm_ref, bf16[2,4,73728]{2,1,0:T(4,128)(2,1)} %query_ref.1, bf16[4,128,640]{2,1,0:T(8,128)(2,1)} %pad.8.fresh_ref), custom_call_target="tpu_custom_call" | custom-call | flops 4000000000 | bytes 8000000 | tf_op jit(solution)/shard_map/attend/pallas_call | solution.py:755
  106.2 0.0 copy-done
  106.3 0.2 reshape.109
  106.4 0.8 copy.32
  107.2 0.0 copy-done.1
  107.2 0.6 reshape.107
  107.8 0.0 copy-done.3
  107.8 0.1 fusion
  107.9 0.6 convert_element_type.42.chosen_ref
  108.5 143.8 %layer.1 = f32[2,8,3584]{2,1,0:T(8,128)} custom-call(bf16[32,32,512]{2,1,0:T(8,128)(2,1)} %attend.1.heads_ref, bf16[4,512,128]{2,1,0:T(8,128)(2,1)} %w_uv_ref.1, f32[2,8,3584]{2,1,0:T(8,128)} %bitcast.23, f32[8,128]{1,0:T(8,128)} %convert_element_type.42.chosen_ref, f32[2,1,3584]{2,1,0:T(1,128)} %bitcast.25, bf16[2,3584,128]{2,1,0:T(8,128)(2,1)} %bitcast.22, ...), custom_call_target="tpu_custom_call" | custom-call | flops 20000000000 | bytes 22000000 | tf_op jit(solution)/shard_map/layer/pallas_call | solution.py:451
  252.3 1.0 convert_bitcast_fusion
  253.2 0.1 copy.28
  253.3 0.7 reshape.106
  (5 shorter events, 0.0 us)
Async XLA Ops:
  0.0 3.5 %copy-start.4 = (s32[1,1,4,20]{3,2,1,0:T(4,128)S(1)}, s32[1,1,4,20]{3,2,1,0:T(4,128)}, u32[]{:S(2)}) copy-start(s32[1,1,4,20]{3,2,1,0:T(4,128)} %param.15) | copy-start | bytes 964
  0.0 5.1 %copy-start.2 = (bf16[2,4,576]{2,1,0:T(4,128)(2,1)S(1)}, bf16[2,4,576]{2,1,0:T(4,128)(2,1)}, u32[]{:S(2)}) copy-start(bf16[2,4,576]{2,1,0:T(4,128)(2,1)} %param.18) | copy-start | bytes 27652
  6.0 100.2 %copy-start = (bf16[2,4,7168]{2,1,0:T(4,128)(2,1)S(1)}, bf16[2,4,7168]{2,1,0:T(4,128)(2,1)}, u32[]{:S(2)}) copy-start(bf16[2,4,7168]{2,1,0:T(4,128)(2,1)} %param.19) | copy-start | bytes 344068
  6.0 101.1 %copy-start.1 = (bf16[7168]{0:T(1024)(128)(2,1)S(1)}, bf16[7168]{0:T(1024)(128)(2,1)}, u32[]{:S(2)}) copy-start(bf16[7168]{0:T(1024)(128)(2,1)} %param.22) | copy-start | bytes 43012
  6.0 101.8 %copy-start.3 = (s32[2,4,8]{2,1,0:T(4,128)S(1)}, s32[2,4,8]{2,1,0:T(4,128)}, u32[]{:S(2)}) copy-start(s32[2,4,8]{2,1,0:T(4,128)} %param.24) | copy-start | bytes 772

commit v4 on v3

--- a/solution.py
+++ b/solution.py
@@ -18,10 +18,18 @@
 HALF = 3584
 GW = HALF + 128
 MESH_IDS = pl.DeviceIdType.MESH
-AG_PARTS = ((0, 640, 640), (1280, 640, 640), (2560, 640, 512))
-RS_PARTS = ((0, 640, 512), (1152, 640, 512), (2304, 640, 640))
-PLANE_PARTS = ((0, 896, 896), (1792, 896, 896))
-COPIES = 160
+AG_PARTS = tuple((640 * i, 384, 256) for i in range(5)) + ((3200, 256, 256),)
+AG_SPLIT = 1920
+RS_PARTS = (
+    (0, 384, 256),
+    (640, 384, 256),
+    (1280, 256, 256),
+    (1792, 384, 256),
+    (2432, 384, 256),
+    (3072, 256, 256),
+)
+PLANE_PARTS = tuple((896 * i, 512, 384) for i in range(4))
+COPIES = 256
 
 
 class Links:
@@ -44,9 +52,14 @@
     def partner(self):
         return (self.z, self.ep + 1 - 2 * self.core)
 
-    def send(self, src, dst, device, landing):
-        k = self.used
-        self.used += 1
+    def take(self, count):
+        first = self.used
+        self.used += count
+        return first
+
+    def send(self, src, dst, device, landing, k=None, start=True):
+        if k is None:
+            k = self.take(1)
         make = lambda s, d: pltpu.make_async_remote_copy(
             src_ref=s,
             dst_ref=d,
@@ -56,7 +69,8 @@
             device_id_type=MESH_IDS,
         )
         out = make(src, dst)
-        out.start()
+        if start:
+            out.start()
         return out, make(landing, landing)
 
 
@@ -75,116 +89,94 @@
     return ref.at[index + (slice(None), pl.ds(start, width))]
 
 
-def gather_blocks(link, held, pushed):
-    sent, pushes = [], []
-
-    def push(part, axis, coord):
-        start, wa, wb = AG_PARTS[part]
-        src = pick(held, {axis: coord}, start, wa + wb)
-        dst = pick(pushed, {axis: coord}, start, wa + wb)
+def gather_part(link, held, pushed, index, sent, pushes):
+    start, wa, wb = AG_PARTS[index]
+    order = [(index + j) % 3 for j in range(3)]
+
+    def push(coord):
+        src = pick(held, {order[2]: coord}, start, wa + wb)
+        dst = pick(pushed, {order[2]: coord}, start, wa + wb)
         pushes.append(link.send(src, dst, link.partner(), dst))
 
     for stage in range(3):
-        first = []
-        for p, (start, wa, wb) in enumerate(AG_PARTS):
-            order = [(p + j) % 3 for j in range(3)]
-            axis = order[stage]
-            rest = {a: link.coords[a] for a in order[stage + 1 :]}
-            mine = pick(held, {**rest, axis: link.coords[axis]}, start, wa + wb)
-            below = pick(held, {**rest, axis: link.shifted(axis, -1)}, start, wa + wb)
-            above = pick(held, {**rest, axis: link.shifted(axis, 1)}, start, wa + wb)
-            first.append(
-                (
-                    link.send(mine, mine, link.neighbour(axis, 1), below),
-                    link.send(mine, mine, link.neighbour(axis, -1), above),
-                )
-            )
-            if stage == 2:
-                push(p, axis, link.coords[axis])
-        second = []
-        for p, (start, wa, wb) in enumerate(AG_PARTS):
-            order = [(p + j) % 3 for j in range(3)]
-            axis = order[stage]
-            rest = {a: link.coords[a] for a in order[stage + 1 :]}
-            wait_in(first[p])
-            up = pick(held, {**rest, axis: link.shifted(axis, -1)}, start, wa)
-            down = pick(held, {**rest, axis: link.shifted(axis, 1)}, start + wa, wb)
-            far_a = pick(held, {**rest, axis: link.shifted(axis, 2)}, start, wa)
-            far_b = pick(held, {**rest, axis: link.shifted(axis, 2)}, start + wa, wb)
-            second.append(
-                (
-                    link.send(up, up, link.neighbour(axis, 1), far_a),
-                    link.send(down, down, link.neighbour(axis, -1), far_b),
-                )
-            )
-            if stage == 2:
-                push(p, axis, link.shifted(axis, -1))
-                push(p, axis, link.shifted(axis, 1))
-        for p in range(3):
-            wait_in(second[p])
-            if stage == 2:
-                push(p, (p + 2) % 3, link.shifted((p + 2) % 3, 2))
-            sent += list(first[p]) + list(second[p])
-    return sent, pushes
-
-
-def scatter_sums(link, parts, axes, sums, landings, last):
-    sent = []
+        axis = order[stage]
+        rest = {a: link.coords[a] for a in order[stage + 1 :]}
+
+        def block(step, lo, w):
+            coord = link.shifted(axis, step) if step else link.coords[axis]
+            return pick(held, {**rest, axis: coord}, lo, w)
+
+        mine = block(0, start, wa + wb)
+        first = (
+            link.send(mine, mine, link.neighbour(axis, 1), block(-1, start, wa + wb)),
+            link.send(mine, mine, link.neighbour(axis, -1), block(1, start, wa + wb)),
+        )
+        if stage == 2:
+            push(link.coords[axis])
+        yield
+        wait_in(first)
+        up, down = block(-1, start, wa), block(1, start + wa, wb)
+        second = (
+            link.send(up, up, link.neighbour(axis, 1), block(2, start, wa)),
+            link.send(down, down, link.neighbour(axis, -1), block(2, start + wa, wb)),
+        )
+        if stage == 2:
+            push(link.shifted(axis, -1))
+            push(link.shifted(axis, 1))
+        sent += list(first) + list(second)
+        yield
+        wait_in(second)
+        if stage == 2:
+            push(link.shifted(axis, 2))
+
+
+def scatter_part(link, parts, index, axes, sums, landings, last, sent):
+    start, wa, wb = parts[index]
     count = len(axes)
+    order = [axes[(index + j) % count] for j in range(count)]
+    f32, bf16 = jnp.float32, jnp.bfloat16
     for stage in range(count):
         far_in, low_in, high_in = landings[stage]
-        steps = []
-        for p, (start, wa, wb) in enumerate(parts):
-            order = [axes[(p + j) % count] for j in range(count)]
-            axis = order[stage]
-            done = {a: link.coords[a] for a in order[:stage]}
-            at = lambda coord, lo, w, done=done, axis=axis: pick(
-                sums, {k - axes[0]: v for k, v in {**done, axis: coord}.items()}, lo, w
-            )
-            land = lambda ref, lo, w: ref.at[(slice(None),) * (count - stage) + (pl.ds(lo, w),)]
-            far = link.shifted(axis, 2)
-            la, lb = land(far_in, start, wa), land(far_in, start + wa, wb)
-            steps.append(
-                (
-                    at,
-                    land,
-                    axis,
-                    (
-                        link.send(at(far, start, wa), la, link.neighbour(axis, 1), la),
-                        link.send(at(far, start + wa, wb), lb, link.neighbour(axis, -1), lb),
-                    ),
-                )
-            )
-        final = []
-        for p, (start, wa, wb) in enumerate(parts):
-            at, land, axis, first = steps[p]
-            wait_in(first)
-            up, down = link.shifted(axis, 1), link.shifted(axis, -1)
-            for coord, lo, w in ((up, start, wa), (down, start + wa, wb)):
-                view, got = at(coord, lo, w), land(far_in, lo, w)
-                view[...] = (
-                    view[...].astype(jnp.float32) + got[...].astype(jnp.float32)
-                ).astype(jnp.bfloat16)
-            low, high = land(low_in, start, wa + wb), land(high_in, start, wa + wb)
-            second = (
-                link.send(at(up, start, wa + wb), low, link.neighbour(axis, 1), low),
-                link.send(at(down, start, wa + wb), high, link.neighbour(axis, -1), high),
-            )
-            final.append((at(link.coords[axis], start, wa + wb), low, high, second))
-            sent += list(first) + list(second)
-        for p, (start, wa, wb) in enumerate(parts):
-            view, low, high, second = final[p]
-            wait_in(second)
-            total = (
-                view[...].astype(jnp.float32)
-                + low[...].astype(jnp.float32)
-                + high[...].astype(jnp.float32)
-            )
-            if stage == count - 1:
-                last(start, wa + wb, total)
-            else:
-                view[...] = total.astype(jnp.bfloat16)
-    return sent
+        axis = order[stage]
+        done = {a: link.coords[a] for a in order[:stage]}
+
+        def at(coord, lo, w):
+            return pick(sums, {k - axes[0]: v for k, v in {**done, axis: coord}.items()}, lo, w)
+
+        def land(ref, lo, w):
+            return ref.at[(slice(None),) * (count - stage) + (pl.ds(lo, w),)]
+
+        far = link.shifted(axis, 2)
+        la, lb = land(far_in, start, wa), land(far_in, start + wa, wb)
+        first = (
+            link.send(at(far, start, wa), la, link.neighbour(axis, 1), la),
+            link.send(at(far, start + wa, wb), lb, link.neighbour(axis, -1), lb),
+        )
+        yield
+        wait_in(first)
+        up, down = link.shifted(axis, 1), link.shifted(axis, -1)
+        for coord, lo, w in ((up, start, wa), (down, start + wa, wb)):
+            view, got = at(coord, lo, w), land(far_in, lo, w)
+            view[...] = (view[...].astype(f32) + got[...].astype(f32)).astype(bf16)
+        low, high = land(low_in, start, wa + wb), land(high_in, start, wa + wb)
+        second = (
+            link.send(at(up, start, wa + wb), low, link.neighbour(axis, 1), low),
+            link.send(at(down, start, wa + wb), high, link.neighbour(axis, -1), high),
+        )
+        sent += list(first) + list(second)
+        yield
+        wait_in(second)
+        view = at(link.coords[axis], start, wa + wb)
+        total = view[...].astype(f32) + low[...].astype(f32) + high[...].astype(f32)
+        if stage == count - 1:
+            last(start, wa + wb, total)
+        else:
+            view[...] = total.astype(bf16)
+
+
+def resume(threads):
+    for thread in threads:
+        next(thread, None)
 
 
 def layer_kernel(
@@ -213,6 +205,7 @@
     plane_b1,
     plane_c0,
     plane_c1,
+    resid_out,
     hid,
     picked,
     stat_out,
@@ -254,11 +247,6 @@
 
     load(w_out_hbm.at[:, :, :, :, other_cols], big.at[pl.ds(2, 2)])
     load(w_out_hbm.at[:, :, :, :, own_cols], big.at[pl.ds(0, 2)])
-    for slot, cols in ((0, own_cols), (1, other_cols)):
-        load(w_gate_hbm.at[cols], wg.at[slot])
-        load(w_up_hbm.at[cols], wu.at[slot])
-        load(w_down_hbm.at[:, cols], wd.at[slot])
-
     barrier = pltpu.get_barrier_semaphore()
     for axis in range(3):
         for step in (1, -1):
@@ -268,9 +256,13 @@
     pl.semaphore_signal(barrier, inc=1, device_id=partner, device_id_type=MESH_IDS)
     pl.semaphore_wait(barrier, 7)
 
+    def token_rows(cols):
+        return jnp.concatenate([resid_ref[s, :, cols].astype(f32) for s in range(2)], axis=0)
+
+    resid_out[...] = token_rows(other_cols)
     sent = []
     swaps = [
-        link.send(resid_ref.at[other], hid.at[core], partner, hid.at[other]),
+        link.send(resid_out, hid.at[core], partner, hid.at[other]),
         link.send(chosen_ref, picked.at[core], partner, picked.at[other]),
     ]
     sent += swaps
@@ -284,35 +276,31 @@
             flat[:, pl.ds(head * 128, 128)] = value.astype(bf16)
 
     def project(slot, start):
-        lanes = pl.ds(start, 256)
-        weight = big[pl.ds(2 * slot, 2), :, :, :, lanes].reshape(512, 256)
+        lanes = pl.ds(start, 896)
+        weight = big[pl.ds(2 * slot, 2), :, :, :, lanes].reshape(512, 896)
         value = jnp.dot(flat[...], weight, preferred_element_type=f32)
-        return value.reshape(4, 4, 16, 256)
+        return value.reshape(4, 4, 16, 896)
 
     loads[0].wait()
     core_swap = []
     for start in (0, 1792):
 
-        @pl.loop(0, 7)
+        @pl.loop(0, 2)
         def _(j, start=start):
-            at = pl.multiple_of(start + j * 256, 256)
-            part_send[:, :, :, pl.ds(at, 256)] = project(1, at).astype(bf16)
+            at = pl.multiple_of(start + j * 896, 128)
+            part_send[:, :, :, pl.ds(at, 896)] = project(1, at).astype(bf16)
 
         lanes = pl.ds(start, 1792)
         dst = part_land.at[:, :, :, lanes]
         core_swap.append(link.send(part_send.at[:, :, :, lanes], dst, partner, dst))
     sent += core_swap
     loads[1].wait()
-    for turn, start in enumerate((0, 1792)):
-        wait_in(core_swap[turn : turn + 1])
-
-        @pl.loop(0, 7)
-        def _(j, start=start):
-            at = pl.multiple_of(start + j * 256, 256)
-            value = project(0, at) + part_land[:, :, :, pl.ds(at, 256)].astype(f32)
-            part_sum[:, :, :, pl.ds(at, 256)] = value.astype(bf16)
-
-    hid[core] = resid_ref[core]
+    for slot, cols in ((0, own_cols), (1, other_cols)):
+        load(w_gate_hbm.at[cols], wg.at[slot])
+        load(w_up_hbm.at[cols], wu.at[slot])
+        load(w_down_hbm.at[:, cols], wd.at[slot])
+
+    hid[core] = token_rows(own_cols)
     picked[core] = chosen_ref[...]
     wait_in(swaps)
 
@@ -320,20 +308,36 @@
         lanes = pl.ds(start, width)
         hid[:, :, lanes] = hid[:, :, lanes] + total.reshape(2, 8, width)
 
-    sent += scatter_sums(
-        link,
-        PLANE_PARTS,
-        (1, 2),
-        part_sum,
-        ((plane_a0, plane_b0, plane_c0), (plane_a1, plane_b1, plane_c1)),
-        add_hidden,
-    )
+    plane_land = ((plane_a0, plane_b0, plane_c0), (plane_a1, plane_b1, plane_c1))
+    threads = []
+    for turn, start in enumerate((0, 1792)):
+        wait_in(core_swap[turn : turn + 1])
+
+        @pl.loop(0, 2)
+        def _(j, start=start):
+            at = pl.multiple_of(start + j * 896, 128)
+            value = project(0, at) + part_land[:, :, :, pl.ds(at, 896)].astype(f32)
+            part_sum[:, :, :, pl.ds(at, 896)] = value.astype(bf16)
+
+        for index in (2 * turn, 2 * turn + 1):
+            threads.append(
+                scatter_part(
+                    link, PLANE_PARTS, index, (1, 2), part_sum, plane_land, add_hidden, sent
+                )
+            )
+            next(threads[-1])
+    for _ in range(4):
+        resume(threads)
 
     hidden = hid[...].reshape(16, HALF)
     gain = gain_ref[core]
-    logits = jnp.dot(
-        (hidden * gain).astype(bf16), router_ref[core], preferred_element_type=f32
+    logits = lax.dot_general(
+        (hidden * gain).astype(bf16),
+        router_ref[:, own_cols],
+        (((1,), (1,)), ((), ())),
+        preferred_element_type=f32,
     )
+    logits = jnp.concatenate([logits, jnp.zeros((16, 96), f32)], axis=1)
     squares = jnp.sum(hidden * hidden, axis=1, keepdims=True)
     lane = lax.broadcasted_iota(jnp.int32, (16, 128), 1)
     mine = jnp.where(lane < 64, logits, jnp.broadcast_to(squares, (16, 128)))
@@ -352,15 +356,29 @@
     held[link.z, link.y, link.x, :, pl.ds(0, HALF)] = normed
     held[link.z, link.y, link.x, :, pl.ds(HALF, 128)] = table.astype(bf16)
 
-    gathers, pushes = gather_blocks(link, held, pushed)
-
+    gathers, pushes = [], []
+    threads = [gather_part(link, held, pushed, i, gathers, pushes) for i in range(6)]
+    for _ in range(6):
+        resume(threads)
+    resume(threads[:3])
     for copy in loads[2:]:
         copy.wait()
 
+    def own_first(i, carry):
+        rows = held[i, :, :, :, pl.ds(0, AG_SPLIT)].reshape(256, AG_SPLIT)
+        cut = pl.ds(0, AG_SPLIT)
+        gate_acc[i] = jnp.dot(rows, wg[0, cut], preferred_element_type=f32)
+        up_acc[i] = jnp.dot(rows, wu[0, cut], preferred_element_type=f32)
+        return carry
+
+    lax.fori_loop(0, 4, own_first, 0)
+    resume(threads[3:])
+
     def own_half(i, carry):
-        rows = held[i, :, :, :, pl.ds(0, HALF)].reshape(256, HALF)
-        gate_acc[i] = jnp.dot(rows, wg[0], preferred_element_type=f32)
-        up_acc[i] = jnp.dot(rows, wu[0], preferred_element_type=f32)
+        cut = pl.ds(AG_SPLIT, HALF - AG_SPLIT)
+        rows = held[i, :, :, :, cut].reshape(256, HALF - AG_SPLIT)
+        gate_acc[i] += jnp.dot(rows, wg[0, cut], preferred_element_type=f32)
+        up_acc[i] += jnp.dot(rows, wu[0, cut], preferred_element_type=f32)
         return carry
 
     lax.fori_loop(0, 4, own_half, 0)
@@ -380,50 +398,67 @@
     lax.fori_loop(0, 4, other_half, 0)
     wait_out(gathers + pushes)
 
-    back = []
-    for i in range(4):
-
-        @pl.loop(0, 7)
-        def _(j, i=i):
-            lanes = pl.ds(pl.multiple_of(j * 512, 512), 512)
-            value = jnp.dot(units[i], wd[1, :, lanes], preferred_element_type=f32)
-            pushed[i, :, :, :, lanes] = value.astype(bf16).reshape(4, 4, 16, 512)
-
-        dst = big.at[i]
-        back.append(link.send(pushed.at[i, :, :, :, pl.ds(0, HALF)], dst, partner, dst))
-    for i in range(4):
-        wait_in(back[i : i + 1])
-
-        @pl.loop(0, 7)
-        def _(j, i=i):
-            lanes = pl.ds(pl.multiple_of(j * 512, 512), 512)
-            value = jnp.dot(units[i], wd[0, :, lanes], preferred_element_type=f32)
-            value = value.reshape(4, 4, 16, 512) + big[i, :, :, :, lanes].astype(f32)
-            held[i, :, :, :, lanes] = value.astype(bf16)
-
-    sent += back
+    def routed_chunk(slot, i, at):
+        weight = wd[slot, :, pl.ds(at, 896)]
+        value = jnp.dot(units[i], weight, preferred_element_type=f32)
+        return value.reshape(4, 4, 16, 896)
+
+    back_first = link.take(8)
+
+    def back(turn, i, start):
+        lanes = pl.ds(1792 * turn, 1792)
+        dst = big.at[i, :, :, :, lanes]
+        k = back_first + 4 * turn + i
+        return link.send(pushed.at[i, :, :, :, lanes], dst, partner, dst, k, start)
+
+    for turn in range(2):
+
+        @pl.loop(0, 4)
+        def _(i, turn=turn):
+            for at in (1792 * turn, 1792 * turn + 896):
+                pushed[i, :, :, :, pl.ds(at, 896)] = routed_chunk(1, i, at).astype(bf16)
+            back(turn, i, True)
 
     def add_routed(start, width, total):
         lanes = pl.ds(start, width)
         fin[:, :, lanes] = hid[:, :, lanes] + total.reshape(2, 8, width)
 
-    sent += scatter_sums(
-        link,
-        RS_PARTS,
-        (0, 1, 2),
-        held,
-        ((far0, low0, high0), (far1, low1, high1), (far2, low2, high2)),
-        add_routed,
-    )
+    torus_land = ((far0, low0, high0), (far1, low1, high1), (far2, low2, high2))
+    threads = []
+    for turn in range(2):
+
+        @pl.loop(0, 4)
+        def _(i, turn=turn):
+            wait_in([back(turn, i, False)])
+            for at in (1792 * turn, 1792 * turn + 896):
+                value = routed_chunk(0, i, at) + big[i, :, :, :, pl.ds(at, 896)].astype(f32)
+                held[i, :, :, :, pl.ds(at, 896)] = value.astype(bf16)
+
+        for index in range(3 * turn, 3 * turn + 3):
+            threads.append(
+                scatter_part(
+                    link, RS_PARTS, index, (0, 1, 2), held, torus_land, add_routed, sent
+                )
+            )
+            next(threads[-1])
+    for _ in range(6):
+        resume(threads)
     swap = link.send(fin.at[other], fin_in, partner, fin_in)
     sent.append(swap)
-    out_ref[core] = fin[core]
+    for s in range(2):
+        out_ref[s, :, own_cols] = fin[core, pl.ds(4 * s, 4)].astype(bf16)
     wait_in([swap])
-    out_ref[other] = fin_in[...]
+    for s in range(2):
+        out_ref[s, :, other_cols] = fin_in[pl.ds(4 * s, 4)].astype(bf16)
     wait_out(sent)
-
-
-def layer_call(head_rows, w_uv, resid_halves, chosen, gain, router, w_out, w_gate, w_up, w_down):
+    for turn in range(2):
+
+        @pl.loop(0, 4)
+        def _(i, turn=turn):
+            wait_out([back(turn, i, False)])
+
+
+def layer_call(head_rows, w_uv, resid, chosen, gain, router, w_out, w_gate, w_up, w_down):
     vmem, hbm = pl.BlockSpec(memory_space=pltpu.VMEM), pl.BlockSpec(memory_space=pl.ANY)
     bf16, f32 = jnp.bfloat16, jnp.float32
 
@@ -438,7 +473,7 @@
         + [pltpu.VMEM((2, 256, HALF), bf16), pltpu.VMEM((256, 512), bf16)]
         + [block(4, 4, 16)] * 3
         + plane
-        + [block(2, 8, kind=f32), pltpu.VMEM((2, 8, 128), f32)]
+        + [block(8, kind=f32), block(2, 8, kind=f32), pltpu.VMEM((2, 8, 128), f32)]
         + [pltpu.VMEM((16, 128), f32)] * 2
         + [block(4, 4, 4, 16, lanes=GW)] * 2
         + [pltpu.VMEM((4, 256, 256), f32)] * 2
@@ -450,7 +485,7 @@
     )
     return pl.pallas_call(
         layer_kernel,
-        out_shape=jax.ShapeDtypeStruct((2, 8, HALF), f32),
+        out_shape=jax.ShapeDtypeStruct((2, 4, 2 * HALF), bf16),
         in_specs=[vmem] * 6 + [hbm] * 4,
         out_specs=vmem,
         scratch_shapes=scratch,
@@ -461,20 +496,18 @@
             flops=20_000_000_000, bytes_accessed=22_000_000, transcendentals=300_000
         ),
         name="layer",
-    )(head_rows, w_uv, resid_halves, chosen, gain, router, w_out, w_gate, w_up, w_down)
+    )(head_rows, w_uv, resid, chosen, gain, router, w_out, w_gate, w_up, w_down)
 
 
 def layer_operands(resid, routes, w_out, norm_gain, router_w, w_gate, w_up, w_down):
-    resid_halves = jnp.swapaxes(resid.reshape(8, 2, HALF), 0, 1).astype(jnp.float32)
     route_rows = routes.reshape(8, -1)
     chosen = jnp.any(route_rows[..., None] == jnp.arange(128), axis=1).astype(jnp.float32)
     gain = norm_gain.astype(jnp.float32).reshape(2, 1, HALF)
-    router = jnp.pad(router_w, ((0, 0), (0, 128 - router_w.shape[1]))).reshape(2, HALF, 128)
     return (
-        resid_halves,
+        resid,
         chosen,
         gain,
-        router,
+        router_w.T,
         w_out.reshape(2, 4, 4, 16, 2 * HALF),
         w_gate[0],
         w_up[0],
@@ -496,6 +529,7 @@
     query_ref,
     fresh_ref,
     heads_ref,
+    fresh_rows,
     raw,
     rows_raw,
     packed,
@@ -626,9 +660,16 @@
     scale = (NOPE + ROPE) ** (-0.5)
     contract = (((1,), (1,)), ((), ()))
 
+    drawn = [fresh_ref[j].astype(f32) for j in range(2)]
+    for q in range(4):
+        rows = jnp.concatenate([one[q : q + 1] for one in drawn] + [jnp.zeros((6, LATW), f32)], 0)
+        rows = jnp.concatenate([rows, jnp.zeros((8, WIDE - LATW), f32)], axis=1)
+        rows = jnp.concatenate([rows, jnp.zeros((120, WIDE), f32)], axis=0)
+        fresh_rows[q] = rows.astype(bf16)
+
     @pl.loop(0, 4)
     def _(q):
-        fresh = fresh_ref[q]
+        fresh = fresh_rows[q]
         score = (
             lax.dot_general(query_even[q], fresh, contract, preferred_element_type=f32) * scale
         )
@@ -750,7 +791,6 @@
     slot_hit = (page_map.reshape(4, 1, 5, 1, 4) == wanted[:, :, None, None, None]).astype(bf16)
     same = jnp.eye(4, dtype=bf16)[:, None, None, :, None]
     perm = (slot_hit[:, None] * same).reshape(4, 128, 80)
-    fresh = jnp.pad(jnp.swapaxes(new_latent, 0, 1), ((0, 0), (0, 126), (0, WIDE - LATW)))
     vmem, hbm = pl.BlockSpec(memory_space=pltpu.VMEM), pl.BlockSpec(memory_space=pl.ANY)
     return pl.pallas_call(
         attend_kernel,
@@ -758,6 +798,7 @@
         in_specs=[pl.BlockSpec(memory_space=pltpu.SMEM), hbm, vmem, vmem, vmem],
         out_specs=vmem,
         scratch_shapes=[
+            pltpu.VMEM((4, 128, WIDE), bf16),
             pltpu.VMEM((slots, 4, width), bf16),
             pltpu.VMEM((PAIR // 128, 320, 128), f32),
             pltpu.VMEM((4, 80, QUARTER), bf16),
@@ -786,7 +827,7 @@
             flops=4_000_000_000, bytes_accessed=8_000_000, transcendentals=1_500_000
         ),
         name="attend",
-    )(prompt_len, jnp.swapaxes(prefill_pages[0, 0], 0, 1), perm, queries, fresh)
+    )(prompt_len, jnp.swapaxes(prefill_pages[0, 0], 0, 1), perm, queries, new_latent)
 
 
 def per_device(
@@ -807,9 +848,7 @@
 ):
     head_rows = attend_call(prefill_pages, page_map, prompt_len, queries, new_latent)
     operands = layer_operands(resid, routes, w_out, norm_gain, router_w, w_gate, w_up, w_down)
-    halves = layer_call(head_rows, w_uv, *operands)
-    rows = jnp.swapaxes(halves, 0, 1).astype(jnp.bfloat16)
-    return rows.reshape(resid.shape)
+    return layer_call(head_rows, w_uv, *operands)
 
 
 def solution(mesh):

time: 254 us -> 234 us (0.921)
  Pallas kernels: 244 us -> 229 us
  local copies, waits for them, and re-layouts: 6.92 us -> 3.07 us
    pallas_call x1, Pallas kernels: 144 us -> 129 us  [layer_call(): pl.pallas_call(layer_kernel, out_shape=jax.ShapeDtypeStruct((2, 4, 2 * HA...]
where the time goes in v4:
time: 234 us
  Pallas kernels  229 us (98%)
  local copies, waits for them, and re-layouts  3.07 us (1%)
    pallas_call x1, Pallas kernels, layer_call(): pl.pallas_call(layer_kernel, out_shape=jax.ShapeDtypeStruct((2, 4, 2 * HA...  129 us
    pallas_call x1, Pallas kernels, attend_call(): pl.pallas_call(attend_kernel, out_shape=jax.ShapeDtypeStruct((32, 32, LAT...  100 us

profile of v4, /device:TPU:1, one launch (start us, length us, event | category | flops | bytes accessed | tf_op | source)
XLA Modules:
  0.0 234.1 jit_solution(8875103784306994806)
XLA Ops:
  0.0 0.8 eq.45
  0.8 0.1 compare_convert_fusion
  0.9 0.1 mul.46
  1.0 0.2 mul.47
  1.2 0.1 copy.18
  1.3 0.1 mul.48
  1.4 0.1 mul.49
  1.5 0.1 copy.17
  1.7 0.7 broadcast_multiply_fusion.perm_ref
  2.3 0.0 copy-start
  2.3 0.0 copy-start.1
  2.3 100.0 %attend.1.heads_ref = bf16[32,32,512]{2,1,0:T(8,128)(2,1)} custom-call(s32[4]{0:T(128)} %length_ref.1, bf16[20,4,36864]{2,1,0:T(4,128)(2,1)} %bitcast.17, bf16[4,128,80]{2,1,0:T(8,128)(2,1)} %broadcast_multiply_fusion.perm_ref, bf16[2,4,73728]{2,1,0:T(4,128)(2,1)} %query_ref.1, bf16[2,4,576]{2,1,0:T(4,128)(2,1)} %fresh_ref.1), custom_call_target="tpu_custom_call" | custom-call | flops 4000000000 | bytes 8000000 | tf_op jit(solution)/shard_map/attend/pallas_call | solution.py:795
  102.3 0.0 copy-done
  102.3 0.6 reshape.96
  102.9 0.0 copy-done.1
  102.9 0.1 fusion
  103.0 0.6 convert_element_type.22.chosen_ref
  103.6 128.8 %layer.1 = bf16[2,4,7168]{2,1,0:T(4,128)(2,1)} custom-call(bf16[32,32,512]{2,1,0:T(8,128)(2,1)} %attend.1.heads_ref, bf16[4,512,128]{2,1,0:T(8,128)(2,1)} %w_uv_ref.1, bf16[2,4,7168]{2,1,0:T(4,128)(2,1)} %resid_ref.1, f32[8,128]{1,0:T(8,128)} %convert_element_type.22.chosen_ref, f32[2,1,3584]{2,1,0:T(1,128)} %bitcast.14, bf16[32,7168]{1,0:T(8,128)(2,1)} %bitcast.21, ...), custom_call_target="tpu_custom_call" | custom-call | flops 20000000000 | bytes 22000000 | tf_op jit(solution)/shard_map/layer/pallas_call | solution.py:486
  232.5 1.6 copy.20
  (4 shorter events, 0.0 us)
Async XLA Ops:
  2.3 100.0 %copy-start = (bf16[7168]{0:T(1024)(128)(2,1)S(1)}, bf16[7168]{0:T(1024)(128)(2,1)}, u32[]{:S(2)}) copy-start(bf16[7168]{0:T(1024)(128)(2,1)} %param.22) | copy-start | bytes 43012
  2.3 100.6 %copy-start.1 = (s32[2,4,8]{2,1,0:T(4,128)S(1)}, s32[2,4,8]{2,1,0:T(4,128)}, u32[]{:S(2)}) copy-start(s32[2,4,8]{2,1,0:T(4,128)} %param.24) | copy-start | bytes 772

commit v5 on v4

--- a/solution.py
+++ b/solution.py
@@ -20,15 +20,16 @@
 MESH_IDS = pl.DeviceIdType.MESH
 AG_PARTS = tuple((640 * i, 384, 256) for i in range(5)) + ((3200, 256, 256),)
 AG_SPLIT = 1920
+GENERATIONS = ((0, 896), (896, 2688))
 RS_PARTS = (
-    (0, 384, 256),
-    (640, 384, 256),
-    (1280, 256, 256),
-    (1792, 384, 256),
-    (2432, 384, 256),
-    (3072, 256, 256),
+    (0, 128, 128),
+    (256, 128, 128),
+    (512, 256, 128),
+    (896, 512, 384),
+    (1792, 512, 384),
+    (2688, 512, 384),
 )
-PLANE_PARTS = tuple((896 * i, 512, 384) for i in range(4))
+PLANE_PARTS = ((0, 256, 256), (512, 256, 128), (896, 768, 640), (2304, 640, 640))
 COPIES = 256
 
 
@@ -107,6 +108,15 @@
             return pick(held, {**rest, axis: coord}, lo, w)
 
         mine = block(0, start, wa + wb)
+        if stage == 0:
+            near = [
+                link.send(mine, mine, link.neighbour(axis, step), block(-step, start, wa + wb))
+                for step in (2, 1, -1)
+            ]
+            sent += near
+            yield
+            wait_in(near)
+            continue
         first = (
             link.send(mine, mine, link.neighbour(axis, 1), block(-1, start, wa + wb)),
             link.send(mine, mine, link.neighbour(axis, -1), block(1, start, wa + wb)),
@@ -147,6 +157,21 @@
             return ref.at[(slice(None),) * (count - stage) + (pl.ds(lo, w),)]
 
         far = link.shifted(axis, 2)
+        if stage == count - 1:
+            whole = (start, wa + wb)
+            near = []
+            for ref, step in ((far_in, 2), (low_in, 1), (high_in, -1)):
+                place = land(ref, *whole)
+                src = at(link.shifted(axis, step), *whole)
+                near.append(link.send(src, place, link.neighbour(axis, step), place))
+            sent += near
+            yield
+            wait_in(near)
+            total = at(link.coords[axis], *whole)[...].astype(f32)
+            for ref in (far_in, low_in, high_in):
+                total = total + land(ref, *whole)[...].astype(f32)
+            last(start, wa + wb, total)
+            continue
         la, lb = land(far_in, start, wa), land(far_in, start + wa, wb)
         first = (
             link.send(at(far, start, wa), la, link.neighbour(axis, 1), la),
@@ -168,10 +193,7 @@
         wait_in(second)
         view = at(link.coords[axis], start, wa + wb)
         total = view[...].astype(f32) + low[...].astype(f32) + high[...].astype(f32)
-        if stage == count - 1:
-            last(start, wa + wb, total)
-        else:
-            view[...] = total.astype(bf16)
+        view[...] = total.astype(bf16)
 
 
 def resume(threads):
@@ -249,12 +271,40 @@
     load(w_out_hbm.at[:, :, :, :, own_cols], big.at[pl.ds(0, 2)])
     barrier = pltpu.get_barrier_semaphore()
     for axis in range(3):
-        for step in (1, -1):
+        for step in (1, -1, 2):
             pl.semaphore_signal(
                 barrier, inc=1, device_id=link.neighbour(axis, step), device_id_type=MESH_IDS
             )
     pl.semaphore_signal(barrier, inc=1, device_id=partner, device_id_type=MESH_IDS)
-    pl.semaphore_wait(barrier, 7)
+
+    for pair in range(2):
+        rows = heads_ref[:, pl.ds(pair * 16, 16), :].reshape(512, LAT)
+        for one in range(2):
+            head = 2 * pair + one
+            value = jnp.dot(rows, w_uv_ref[head], preferred_element_type=f32)
+            value = value.reshape(32, 2, 8, 128)[:, one].reshape(256, 128)
+            flat[:, pl.ds(head * 128, 128)] = value.astype(bf16)
+
+    def project(slot, start):
+        lanes = pl.ds(start, 896)
+        weight = big[pl.ds(2 * slot, 2), :, :, :, lanes].reshape(512, 896)
+        value = jnp.dot(flat[...], weight, preferred_element_type=f32)
+        return value.reshape(4, 4, 16, 896)
+
+    def project_away(start, width):
+        @pl.loop(0, width // 896)
+        def _(j):
+            at = pl.multiple_of(start + j * 896, 128)
+            part_send[:, :, :, pl.ds(at, 896)] = project(1, at).astype(bf16)
+
+    def swap_sums(start, width):
+        lanes = pl.ds(start, width)
+        dst = part_land.at[:, :, :, lanes]
+        return link.send(part_send.at[:, :, :, lanes], dst, partner, dst)
+
+    loads[0].wait()
+    project_away(*GENERATIONS[0])
+    pl.semaphore_wait(barrier, 10)
 
     def token_rows(cols):
         return jnp.concatenate([resid_ref[s, :, cols].astype(f32) for s in range(2)], axis=0)
@@ -267,32 +317,9 @@
     ]
     sent += swaps
 
-    for pair in range(2):
-        rows = heads_ref[:, pl.ds(pair * 16, 16), :].reshape(512, LAT)
-        for one in range(2):
-            head = 2 * pair + one
-            value = jnp.dot(rows, w_uv_ref[head], preferred_element_type=f32)
-            value = value.reshape(32, 2, 8, 128)[:, one].reshape(256, 128)
-            flat[:, pl.ds(head * 128, 128)] = value.astype(bf16)
-
-    def project(slot, start):
-        lanes = pl.ds(start, 896)
-        weight = big[pl.ds(2 * slot, 2), :, :, :, lanes].reshape(512, 896)
-        value = jnp.dot(flat[...], weight, preferred_element_type=f32)
-        return value.reshape(4, 4, 16, 896)
-
-    loads[0].wait()
-    core_swap = []
-    for start in (0, 1792):
-
-        @pl.loop(0, 2)
-        def _(j, start=start):
-            at = pl.multiple_of(start + j * 896, 128)
-            part_send[:, :, :, pl.ds(at, 896)] = project(1, at).astype(bf16)
-
-        lanes = pl.ds(start, 1792)
-        dst = part_land.at[:, :, :, lanes]
-        core_swap.append(link.send(part_send.at[:, :, :, lanes], dst, partner, dst))
+    core_swap = [swap_sums(*GENERATIONS[0])]
+    project_away(*GENERATIONS[1])
+    core_swap.append(swap_sums(*GENERATIONS[1]))
     sent += core_swap
     loads[1].wait()
     for slot, cols in ((0, own_cols), (1, other_cols)):
@@ -310,10 +337,10 @@
 
     plane_land = ((plane_a0, plane_b0, plane_c0), (plane_a1, plane_b1, plane_c1))
     threads = []
-    for turn, start in enumerate((0, 1792)):
+    for turn, (start, width) in enumerate(GENERATIONS):
         wait_in(core_swap[turn : turn + 1])
 
-        @pl.loop(0, 2)
+        @pl.loop(0, width // 896)
         def _(j, start=start):
             at = pl.multiple_of(start + j * 896, 128)
             value = project(0, at) + part_land[:, :, :, pl.ds(at, 896)].astype(f32)
@@ -326,7 +353,7 @@
                 )
             )
             next(threads[-1])
-    for _ in range(4):
+    for _ in range(3):
         resume(threads)
 
     hidden = hid[...].reshape(16, HALF)
@@ -358,7 +385,7 @@
 
     gathers, pushes = [], []
     threads = [gather_part(link, held, pushed, i, gathers, pushes) for i in range(6)]
-    for _ in range(6):
+    for _ in range(5):
         resume(threads)
     resume(threads[:3])
     for copy in loads[2:]:
@@ -403,10 +430,11 @@
         value = jnp.dot(units[i], weight, preferred_element_type=f32)
         return value.reshape(4, 4, 16, 896)
 
+    chunks = [range(start, start + width, 896) for start, width in GENERATIONS]
     back_first = link.take(8)
 
     def back(turn, i, start):
-        lanes = pl.ds(1792 * turn, 1792)
+        lanes = pl.ds(*GENERATIONS[turn])
         dst = big.at[i, :, :, :, lanes]
         k = back_first + 4 * turn + i
         return link.send(pushed.at[i, :, :, :, lanes], dst, partner, dst, k, start)
@@ -415,7 +443,7 @@
 
         @pl.loop(0, 4)
         def _(i, turn=turn):
-            for at in (1792 * turn, 1792 * turn + 896):
+            for at in chunks[turn]:
                 pushed[i, :, :, :, pl.ds(at, 896)] = routed_chunk(1, i, at).astype(bf16)
             back(turn, i, True)
 
@@ -430,7 +458,7 @@
         @pl.loop(0, 4)
         def _(i, turn=turn):
             wait_in([back(turn, i, False)])
-            for at in (1792 * turn, 1792 * turn + 896):
+            for at in chunks[turn]:
                 value = routed_chunk(0, i, at) + big[i, :, :, :, pl.ds(at, 896)].astype(f32)
                 held[i, :, :, :, pl.ds(at, 896)] = value.astype(bf16)
 
@@ -441,7 +469,7 @@
                 )
             )
             next(threads[-1])
-    for _ in range(6):
+    for _ in range(5):
         resume(threads)
     swap = link.send(fin.at[other], fin_in, partner, fin_in)
     sent.append(swap)
@@ -606,10 +634,8 @@
         device = (z, lax.rem(ep + d, 32))
         pl.semaphore_signal(barrier, inc=1, device_id=device, device_id_type=MESH_IDS)
 
-    pl.semaphore_wait(barrier, 34)
-
-    @pl.loop(0, CHUNKS)
-    def _(j):
+
+    def repack(j):
         for quarter in range(4):
             fetch(j, quarter).wait()
         for quarter in range(4):
@@ -630,9 +656,19 @@
             for k in range(PAIR // 128):
                 column = pl.ds(pl.multiple_of(j * PAIR + k * 128, 128), 128)
                 packed[owner, :, column] = rows_raw[k, pl.ds(owner, 80, stride=4), :].astype(bf16)
-        own(j).start()
+
+    repack(0)
+    pl.semaphore_wait(barrier, 34)
+
+    @pl.loop(0, CHUNKS)
+    def _(j):
         for kind in range(3):
             outgoing(kind, j).start()
+        own(j).start()
+
+        @pl.when(j + 1 < CHUNKS)
+        def _():
+            repack(j + 1)
 
     @pl.loop(0, 64)
     def _(pair):

time: 234 us -> 230 us (0.983)
  Pallas kernels: 229 us -> 224 us
    pallas_call x1, Pallas kernels: 129 us -> 125 us  [layer_call(): pl.pallas_call(layer_kernel, out_shape=jax.ShapeDtypeStruct((2, 4, 2 * HA...]
where the time goes in v5:
time: 230 us
  Pallas kernels  224 us (97%)
  local copies, waits for them, and re-layouts  3.07 us (1%)
    pallas_call x1, Pallas kernels, layer_call(): pl.pallas_call(layer_kernel, out_shape=jax.ShapeDtypeStruct((2, 4, 2 * HA...  125 us
    pallas_call x1, Pallas kernels, attend_call(): pl.pallas_call(attend_kernel, out_shape=jax.ShapeDtypeStruct((32, 32, LAT...  99.5 us

profile of v5, /device:TPU:1, one launch (start us, length us, event | category | flops | bytes accessed | tf_op | source)
XLA Modules:
  0.0 229.6 jit_solution(7714136102376355745)
XLA Ops:
  0.0 0.8 eq.45
  0.8 0.1 compare_convert_fusion
  0.9 0.1 mul.46
  1.0 0.2 mul.47
  1.2 0.1 copy.18
  1.3 0.1 mul.48
  1.4 0.1 mul.49
  1.5 0.1 copy.17
  1.7 0.7 broadcast_multiply_fusion.perm_ref
  2.3 0.0 copy-start
  2.3 0.0 copy-start.1
  2.3 99.5 %attend.1.heads_ref = bf16[32,32,512]{2,1,0:T(8,128)(2,1)} custom-call(s32[4]{0:T(128)} %length_ref.1, bf16[20,4,36864]{2,1,0:T(4,128)(2,1)} %bitcast.17, bf16[4,128,80]{2,1,0:T(8,128)(2,1)} %broadcast_multiply_fusion.perm_ref, bf16[2,4,73728]{2,1,0:T(4,128)(2,1)} %query_ref.1, bf16[2,4,576]{2,1,0:T(4,128)(2,1)} %fresh_ref.1), custom_call_target="tpu_custom_call" | custom-call | flops 4000000000 | bytes 8000000 | tf_op jit(solution)/shard_map/attend/pallas_call | solution.py:831
  101.8 0.0 copy-done
  101.9 0.6 reshape.96
  102.5 0.0 copy-done.1
  102.5 0.1 fusion
  102.6 0.6 convert_element_type.22.chosen_ref
  103.2 124.9 %layer.1 = bf16[2,4,7168]{2,1,0:T(4,128)(2,1)} custom-call(bf16[32,32,512]{2,1,0:T(8,128)(2,1)} %attend.1.heads_ref, bf16[4,512,128]{2,1,0:T(8,128)(2,1)} %w_uv_ref.1, bf16[2,4,7168]{2,1,0:T(4,128)(2,1)} %resid_ref.1, f32[8,128]{1,0:T(8,128)} %convert_element_type.22.chosen_ref, f32[2,1,3584]{2,1,0:T(1,128)} %bitcast.14, bf16[32,7168]{1,0:T(8,128)(2,1)} %bitcast.21, ...), custom_call_target="tpu_custom_call" | custom-call | flops 20000000000 | bytes 22000000 | tf_op jit(solution)/shard_map/layer/pallas_call | solution.py:514
  228.1 1.6 copy.20
  (4 shorter events, 0.0 us)
Async XLA Ops:
  2.3 99.5 %copy-start = (bf16[7168]{0:T(1024)(128)(2,1)S(1)}, bf16[7168]{0:T(1024)(128)(2,1)}, u32[]{:S(2)}) copy-start(bf16[7168]{0:T(1024)(128)(2,1)} %param.22) | copy-start | bytes 43012
  2.3 100.2 %copy-start.1 = (s32[2,4,8]{2,1,0:T(4,128)S(1)}, s32[2,4,8]{2,1,0:T(4,128)}, u32[]{:S(2)}) copy-start(s32[2,4,8]{2,1,0:T(4,128)} %param.24) | copy-start | bytes 772

commit v6 on v5

--- a/solution.py
+++ b/solution.py
@@ -205,7 +205,7 @@
     heads_ref,
     w_uv_ref,
     resid_ref,
-    chosen_ref,
+    routes_ref,
     gain_ref,
     router_ref,
     w_out_hbm,
@@ -227,6 +227,7 @@
     plane_b1,
     plane_c0,
     plane_c1,
+    mask_out,
     resid_out,
     hid,
     picked,
@@ -310,10 +311,16 @@
         return jnp.concatenate([resid_ref[s, :, cols].astype(f32) for s in range(2)], axis=0)
 
     resid_out[...] = token_rows(other_cols)
+    names = jnp.concatenate([routes_ref[s] for s in range(2)], axis=0)
+    expert = lax.broadcasted_iota(jnp.int32, (8, 128), 1)
+    mask = jnp.zeros((8, 128), f32)
+    for k in range(routes_ref.shape[2]):
+        mask = jnp.where(expert == names[:, k : k + 1], 1.0, mask)
+    mask_out[...] = mask
     sent = []
     swaps = [
         link.send(resid_out, hid.at[core], partner, hid.at[other]),
-        link.send(chosen_ref, picked.at[core], partner, picked.at[other]),
+        link.send(mask_out, picked.at[core], partner, picked.at[other]),
     ]
     sent += swaps
 
@@ -328,7 +335,7 @@
         load(w_down_hbm.at[:, cols], wd.at[slot])
 
     hid[core] = token_rows(own_cols)
-    picked[core] = chosen_ref[...]
+    picked[core] = mask_out[...]
     wait_in(swaps)
 
     def add_hidden(start, width, total):
@@ -392,37 +399,38 @@
         copy.wait()
 
     def own_first(i, carry):
-        rows = held[i, :, :, :, pl.ds(0, AG_SPLIT)].reshape(256, AG_SPLIT)
+        rows = held[pl.ds(4 * i, 4), :, :, :, pl.ds(0, AG_SPLIT)].reshape(1024, AG_SPLIT)
         cut = pl.ds(0, AG_SPLIT)
         gate_acc[i] = jnp.dot(rows, wg[0, cut], preferred_element_type=f32)
         up_acc[i] = jnp.dot(rows, wu[0, cut], preferred_element_type=f32)
         return carry
 
-    lax.fori_loop(0, 4, own_first, 0)
+    lax.fori_loop(0, 1, own_first, 0)
     resume(threads[3:])
 
     def own_half(i, carry):
         cut = pl.ds(AG_SPLIT, HALF - AG_SPLIT)
-        rows = held[i, :, :, :, cut].reshape(256, HALF - AG_SPLIT)
+        rows = held[pl.ds(4 * i, 4), :, :, :, cut].reshape(1024, HALF - AG_SPLIT)
         gate_acc[i] += jnp.dot(rows, wg[0, cut], preferred_element_type=f32)
         up_acc[i] += jnp.dot(rows, wu[0, cut], preferred_element_type=f32)
         return carry
 
-    lax.fori_loop(0, 4, own_half, 0)
+    lax.fori_loop(0, 1, own_half, 0)
     wait_in(pushes)
 
     def other_half(i, carry):
-        rows = pushed[i, :, :, :, pl.ds(0, HALF)].reshape(256, HALF)
+        rows = pushed[pl.ds(4 * i, 4), :, :, :, pl.ds(0, HALF)].reshape(1024, HALF)
         gate_part = gate_acc[i] + jnp.dot(rows, wg[1], preferred_element_type=f32)
         up_part = up_acc[i] + jnp.dot(rows, wu[1], preferred_element_type=f32)
-        table = held[i, :, :, :, pl.ds(HALF, 128)].reshape(256, 128).astype(f32)
-        lane = lax.broadcasted_iota(jnp.int32, (256, 128), 1)
+        table = held[pl.ds(4 * i, 4), :, :, :, pl.ds(HALF, 128)].reshape(1024, 128).astype(f32)
+        lane = lax.broadcasted_iota(jnp.int32, (1024, 128), 1)
         here = (lane == link.ep) | (lane == link.ep + 32)
         factor = jnp.sum(jnp.where(here, table, 0.0), axis=1, keepdims=True)
-        units[i] = (jax.nn.silu(gate_part) * up_part * factor).astype(bf16)
+        value = (jax.nn.silu(gate_part) * up_part * factor).astype(bf16)
+        units[pl.ds(4 * i, 4)] = value.reshape(4, 256, 256)
         return carry
 
-    lax.fori_loop(0, 4, other_half, 0)
+    lax.fori_loop(0, 1, other_half, 0)
     wait_out(gathers + pushes)
 
     def routed_chunk(slot, i, at):
@@ -474,10 +482,10 @@
     swap = link.send(fin.at[other], fin_in, partner, fin_in)
     sent.append(swap)
     for s in range(2):
-        out_ref[s, :, own_cols] = fin[core, pl.ds(4 * s, 4)].astype(bf16)
+        out_ref[s, :, own_cols] = fin[core, pl.ds(4 * s, 4)]
     wait_in([swap])
     for s in range(2):
-        out_ref[s, :, other_cols] = fin_in[pl.ds(4 * s, 4)].astype(bf16)
+        out_ref[s, :, other_cols] = fin_in[pl.ds(4 * s, 4)]
     wait_out(sent)
     for turn in range(2):
 
@@ -486,7 +494,7 @@
             wait_out([back(turn, i, False)])
 
 
-def layer_call(head_rows, w_uv, resid, chosen, gain, router, w_out, w_gate, w_up, w_down):
+def layer_call(head_rows, w_uv, resid, routes, gain, router, w_out, w_gate, w_up, w_down):
     vmem, hbm = pl.BlockSpec(memory_space=pltpu.VMEM), pl.BlockSpec(memory_space=pl.ANY)
     bf16, f32 = jnp.bfloat16, jnp.float32
 
@@ -501,10 +509,10 @@
         + [pltpu.VMEM((2, 256, HALF), bf16), pltpu.VMEM((256, 512), bf16)]
         + [block(4, 4, 16)] * 3
         + plane
-        + [block(8, kind=f32), block(2, 8, kind=f32), pltpu.VMEM((2, 8, 128), f32)]
+        + [pltpu.VMEM((8, 128), f32), block(8, kind=f32), block(2, 8, kind=f32), pltpu.VMEM((2, 8, 128), f32)]
         + [pltpu.VMEM((16, 128), f32)] * 2
         + [block(4, 4, 4, 16, lanes=GW)] * 2
-        + [pltpu.VMEM((4, 256, 256), f32)] * 2
+        + [pltpu.VMEM((1, 1024, 256), f32)] * 2
         + [pltpu.VMEM((4, 256, 256), bf16)]
         + torus
         + [block(2, 8, kind=f32), block(8, kind=f32)]
@@ -513,7 +521,7 @@
     )
     return pl.pallas_call(
         layer_kernel,
-        out_shape=jax.ShapeDtypeStruct((2, 4, 2 * HALF), bf16),
+        out_shape=jax.ShapeDtypeStruct((2, 4, 2 * HALF), f32),
         in_specs=[vmem] * 6 + [hbm] * 4,
         out_specs=vmem,
         scratch_shapes=scratch,
@@ -524,16 +532,14 @@
             flops=20_000_000_000, bytes_accessed=22_000_000, transcendentals=300_000
         ),
         name="layer",
-    )(head_rows, w_uv, resid, chosen, gain, router, w_out, w_gate, w_up, w_down)
+    )(head_rows, w_uv, resid, routes, gain, router, w_out, w_gate, w_up, w_down)
 
 
 def layer_operands(resid, routes, w_out, norm_gain, router_w, w_gate, w_up, w_down):
-    route_rows = routes.reshape(8, -1)
-    chosen = jnp.any(route_rows[..., None] == jnp.arange(128), axis=1).astype(jnp.float32)
     gain = norm_gain.astype(jnp.float32).reshape(2, 1, HALF)
     return (
         resid,
-        chosen,
+        routes,
         gain,
         router_w.T,
         w_out.reshape(2, 4, 4, 16, 2 * HALF),
@@ -548,6 +554,7 @@
 WIDE = 640
 QUARTER = 9216
 SPREAD = (2, 1, 3)
+AHEAD = 4
 
 
 def attend_kernel(
@@ -662,8 +669,11 @@
 
     @pl.loop(0, CHUNKS)
     def _(j):
-        for kind in range(3):
-            outgoing(kind, j).start()
+        @pl.when(j < AHEAD)
+        def _():
+            for kind in range(3):
+                outgoing(kind, j).start()
+
         own(j).start()
 
         @pl.when(j + 1 < CHUNKS)
@@ -721,6 +731,11 @@
 
     @pl.loop(0, CHUNKS)
     def _(j):
+        @pl.when(j + AHEAD < CHUNKS)
+        def _():
+            for kind in range(3):
+                outgoing(kind, j + AHEAD).start()
+
         own(j).wait()
         for kind in range(3):
             arrived(kind, j)
@@ -775,12 +790,10 @@
                     block * 64 : block * 64 + 64, k * 128 : k * 128 + 128
                 ]
 
-    @pl.loop(0, 32)
-    def _(e):
-        for k in range(LAT // 128):
-            out16[e, :, pl.ds(k * 128, 128)] = out32[
-                k, pl.ds(pl.multiple_of(e * 32, 32), 32), :
-            ].astype(bf16)
+    def rounded(e):
+        rows = pl.ds(pl.multiple_of(e * 32, 32), 32)
+        parts = [out32[k, rows, :] for k in range(LAT // 128)]
+        return jnp.concatenate(parts, axis=1).astype(bf16)
 
     def head_copy(d, src, dst, device):
         return pltpu.make_async_remote_copy(
@@ -798,9 +811,11 @@
 
     @pl.loop(1, 32)
     def _(d):
+        target = lax.rem(ep + d, 32)
+        out16[target] = rounded(target)
         head_block(d).start()
 
-    heads_ref[ep] = out16[ep]
+    heads_ref[ep] = rounded(ep)
 
     @pl.loop(1, 32)
     def _(d):
@@ -884,7 +899,7 @@
 ):
     head_rows = attend_call(prefill_pages, page_map, prompt_len, queries, new_latent)
     operands = layer_operands(resid, routes, w_out, norm_gain, router_w, w_gate, w_up, w_down)
-    return layer_call(head_rows, w_uv, *operands)
+    return layer_call(head_rows, w_uv, *operands).astype(jnp.bfloat16)
 
 
 def solution(mesh):

time: 230 us -> 228 us (level)
  no operation moved by 1% of the time
where the time goes in v6:
time: 228 us
  Pallas kernels  222 us (97%)
  other arithmetic  3.73 us (2%)
    pallas_call x1, Pallas kernels, layer_call(): pl.pallas_call(layer_kernel, out_shape=jax.ShapeDtypeStruct((2, 4, 2 * HA...  123 us
    pallas_call x1, Pallas kernels, attend_call(): pl.pallas_call(attend_kernel, out_shape=jax.ShapeDtypeStruct((32, 32, LAT...  99.2 us

profile of v6, /device:TPU:1, one launch (start us, length us, event | category | flops | bytes accessed | tf_op | source)
XLA Modules:
  0.0 227.6 jit_solution(10181931558236840778)
XLA Ops:
  0.0 0.8 eq.30
  0.8 0.1 compare_convert_fusion
  0.9 1.3 reshape.95
  2.2 0.1 mul.48
  2.3 0.1 mul.49
  2.4 0.1 copy.15
  2.5 0.1 mul.46
  2.6 0.2 mul.47
  2.8 0.1 copy.16
  3.0 0.7 broadcast_multiply_fusion.perm_ref
  3.6 99.2 %attend.1.heads_ref = bf16[32,32,512]{2,1,0:T(8,128)(2,1)} custom-call(s32[4]{0:T(128)} %length_ref.1, bf16[20,4,36864]{2,1,0:T(4,128)(2,1)} %bitcast.15, bf16[4,128,80]{2,1,0:T(8,128)(2,1)} %broadcast_multiply_fusion.perm_ref, bf16[2,4,73728]{2,1,0:T(4,128)(2,1)} %query_ref.1, bf16[2,4,576]{2,1,0:T(4,128)(2,1)} %fresh_ref.1), custom_call_target="tpu_custom_call" | custom-call | flops 4000000000 | bytes 8000000 | tf_op jit(solution)/shard_map/attend/pallas_call | solution.py:846
  102.8 123.1 %layer.1 = f32[2,4,7168]{2,1,0:T(4,128)} custom-call(bf16[32,32,512]{2,1,0:T(8,128)(2,1)} %attend.1.heads_ref, bf16[4,512,128]{2,1,0:T(8,128)(2,1)} %w_uv_ref.1, bf16[2,4,7168]{2,1,0:T(4,128)(2,1)} %resid_ref.1, s32[2,4,8]{2,1,0:T(4,128)} %routes_ref.1, f32[2,1,3584]{2,1,0:T(1,128)} %bitcast.13, bf16[32,7168]{1,0:T(8,128)(2,1)} %bitcast.19, ...), custom_call_target="tpu_custom_call" | custom-call | flops 20000000000 | bytes 22000000 | tf_op jit(solution)/shard_map/layer/pallas_call | solution.py:522
  225.9 1.6 convert_element_type.22
  (4 shorter events, 0.0 us)

commit v7 on v6

--- a/solution.py
+++ b/solution.py
@@ -18,8 +18,15 @@
 HALF = 3584
 GW = HALF + 128
 MESH_IDS = pl.DeviceIdType.MESH
-AG_PARTS = tuple((640 * i, 384, 256) for i in range(5)) + ((3200, 256, 256),)
-AG_SPLIT = 1920
+AG_PARTS = (
+    (0, 512, 384),
+    (896, 512, 384),
+    (1792, 384, 384),
+    (2560, 256, 128),
+    (2944, 256, 128),
+    (3328, 256, 128),
+)
+AG_SPLIT = 2560
 GENERATIONS = ((0, 896), (896, 2688))
 RS_PARTS = (
     (0, 128, 128),
@@ -561,9 +568,11 @@
     length_ref,
     pages_hbm,
     perm_ref,
-    query_ref,
+    query_hbm,
     fresh_ref,
     heads_ref,
+    query_ref,
+    query_sem,
     fresh_rows,
     raw,
     rows_raw,
@@ -664,6 +673,8 @@
                 column = pl.ds(pl.multiple_of(j * PAIR + k * 128, 128), 128)
                 packed[owner, :, column] = rows_raw[k, pl.ds(owner, 80, stride=4), :].astype(bf16)
 
+    query_load = pltpu.make_async_copy(query_hbm, query_ref, query_sem)
+    query_load.start()
     repack(0)
     pl.semaphore_wait(barrier, 34)
 
@@ -679,6 +690,8 @@
         @pl.when(j + 1 < CHUNKS)
         def _():
             repack(j + 1)
+
+    query_load.wait()
 
     @pl.loop(0, 64)
     def _(pair):
@@ -846,9 +859,11 @@
     return pl.pallas_call(
         attend_kernel,
         out_shape=jax.ShapeDtypeStruct((32, 32, LAT), bf16),
-        in_specs=[pl.BlockSpec(memory_space=pltpu.SMEM), hbm, vmem, vmem, vmem],
+        in_specs=[pl.BlockSpec(memory_space=pltpu.SMEM), hbm, vmem, hbm, vmem],
         out_specs=vmem,
         scratch_shapes=[
+            pltpu.VMEM(queries.shape, bf16),
+            pltpu.SemaphoreType.DMA,
             pltpu.VMEM((4, 128, WIDE), bf16),
             pltpu.VMEM((slots, 4, width), bf16),
             pltpu.VMEM((PAIR // 128, 320, 128), f32),

time: 228 us -> 229 us (level)
  no operation moved by 1% of the time
where the time goes in v7:
time: 229 us
  Pallas kernels  223 us (97%)
  other arithmetic  3.73 us (2%)
    pallas_call x1, Pallas kernels, layer_call(): pl.pallas_call(layer_kernel, out_shape=jax.ShapeDtypeStruct((2, 4, 2 * HA...  124 us
    pallas_call x1, Pallas kernels, attend_call(): pl.pallas_call(attend_kernel, out_shape=jax.ShapeDtypeStruct((32, 32, LAT...  98.9 us

profile of v7, /device:TPU:1, one launch (start us, length us, event | category | flops | bytes accessed | tf_op | source)
XLA Modules:
  0.0 228.6 jit_solution(18200010229765081857)
XLA Ops:
  0.0 0.8 eq.30
  0.8 0.1 compare_convert_fusion
  0.9 1.3 reshape.95
  2.2 0.1 mul.48
  2.3 0.1 mul.49
  2.4 0.1 copy.15
  2.5 0.1 mul.46
  2.6 0.2 mul.47
  2.8 0.1 copy.16
  3.0 0.7 broadcast_multiply_fusion.perm_ref
  3.6 98.9 %attend.1.heads_ref = bf16[32,32,512]{2,1,0:T(8,128)(2,1)} custom-call(s32[4]{0:T(128)} %length_ref.1, bf16[20,4,36864]{2,1,0:T(4,128)(2,1)} %bitcast.15, bf16[4,128,80]{2,1,0:T(8,128)(2,1)} %broadcast_multiply_fusion.perm_ref, bf16[2,4,73728]{2,1,0:T(4,128)(2,1)} %query_hbm.1, bf16[2,4,576]{2,1,0:T(4,128)(2,1)} %fresh_ref.1), custom_call_target="tpu_custom_call" | custom-call | flops 4000000000 | bytes 8000000 | tf_op jit(solution)/shard_map/attend/pallas_call | solution.py:859
  102.5 124.4 %layer.1 = f32[2,4,7168]{2,1,0:T(4,128)} custom-call(bf16[32,32,512]{2,1,0:T(8,128)(2,1)} %attend.1.heads_ref, bf16[4,512,128]{2,1,0:T(8,128)(2,1)} %w_uv_ref.1, bf16[2,4,7168]{2,1,0:T(4,128)(2,1)} %resid_ref.1, s32[2,4,8]{2,1,0:T(4,128)} %routes_ref.1, f32[2,1,3584]{2,1,0:T(1,128)} %bitcast.13, bf16[32,7168]{1,0:T(8,128)(2,1)} %bitcast.19, ...), custom_call_target="tpu_custom_call" | custom-call | flops 20000000000 | bytes 22000000 | tf_op jit(solution)/shard_map/layer/pallas_call | solution.py:529
  226.9 1.6 convert_element_type.22
  (4 shorter events, 0.0 us)
